TPU v7x, 128 devices: a whole 4x4x4 slice. The times are simulated.
128 devices in a mesh: dp: 16 (over x, z), enc: 8 (over y, core).
Axes of the slice: x: 4, y: 4, z: 4, core: 2. Of those that a mesh axis runs over, the one named last changes fastest.
Arguments:
- tokens: bfloat16 [4096, 4096], P('dp'), may hold values from -10 to 10
- store: bfloat16 [1024, 128, 4096], P(('dp', 'enc')), may hold values from -10 to 10
- holder: int32 [128, 1], P('dp'), may hold values from 0 to 7; in each aligned block of 8 rows (0 to 7, 8 to 15, ...) at most 3 rows name the same one
- rows: int32 [128], P('dp'), may hold values from 0 to 7
- wq: bfloat16 [4096, 2048], P('dp', 'enc'), may hold values from -0.1015625 to 0.1015625
- wk: bfloat16 [4096, 2048], P('dp', 'enc'), may hold values from -0.1015625 to 0.1015625
- wv: bfloat16 [4096, 2048], P('dp', 'enc'), may hold values from -0.09375 to 0.09375
- wo: bfloat16 [2048, 4096], P('enc', 'dp'), may hold values from -0.125 to 0.125
- cotangent: bfloat16 [4096, 4096], P('dp'), may hold values from -6 to 6
Outputs:
- cca_out: bfloat16 [4096, 4096], P('dp', 'enc')
- grad_tokens: bfloat16 [4096, 4096], P('dp', 'enc')
- grad_wq: bfloat16 [4096, 2048], P('dp', 'enc')
- grad_wk: bfloat16 [4096, 2048], P('dp', 'enc')
- grad_wv: bfloat16 [4096, 2048], P('dp', 'enc')
- grad_wo: bfloat16 [2048, 4096], P('enc', 'dp')
Inputs may be any that keep to these rules, and one draw needn't show every extreme that they name: `holder`: in each aligned block of 8 entries (the neighbours of one dp index) no enc index appears more than 3 times; in some blocks one appears exactly 3 times.
All inputs are finite; a program needn't handle non-finite values.
Results may differ from a plain program's by a relative error of at most 0.024.
The roundings to bfloat16 on the way count: a program that leaves them out, or rounds other values in their place, can miss the bound.
Values may be sent and summed in bfloat16 or wider, within the bound.
A program may use at most 128 MiB of HBM per device.

v0:
```python
import math

import jax
import jax.numpy as jnp
from jax import lax
from jax.sharding import PartitionSpec as P

HD = 128
CL = 64
CAP = 3


def rounded(x):
    return lax.optimization_barrier(x.astype(jnp.bfloat16)).astype(jnp.float32)


def body(tokens, store, holder, rows, wq, wk, wv, wo, cotangent):
    me = lax.axis_index("enc")
    scale = 1.0 / math.sqrt(HD)
    nlen = store.shape[1]
    width = store.shape[2]
    wq_full, wk_full, wv_full, wo_full = (
        lax.all_gather(wq, "dp", axis=0, tiled=True),
        lax.all_gather(wk, "dp", axis=0, tiled=True),
        lax.all_gather(wv, "dp", axis=0, tiled=True),
        lax.all_gather(wo, "dp", axis=1, tiled=True),
    )
    owners = holder[:, 0]
    count = owners.shape[0]
    mine = (owners == me).astype(jnp.int32)
    order = jnp.cumsum(mine) - 1
    slot_ids = jnp.arange(CAP, dtype=jnp.int32)
    pick = mine[None, :] * (order[None, :] == slot_ids[:, None]).astype(jnp.int32)
    local_rows = jnp.sum(pick * rows[None, :], axis=1)
    outgoing = jnp.take(store, local_rows, axis=0)
    arrived = lax.all_gather(outgoing, "enc", axis=0, tiled=True)
    places = jnp.arange(count, dtype=jnp.int32)
    earlier = (owners[None, :] == owners[:, None]) & (places[None, :] < places[:, None])
    rank = jnp.sum(earlier.astype(jnp.int32), axis=1)
    neighbours = jnp.take(arrived, owners * CAP + rank, axis=0)
    flat = neighbours.reshape(count * nlen, width)
    tok_rows = tokens.shape[0]
    spans = tok_rows // CL
    local_width = wq_full.shape[1]
    heads_here = local_width // HD
    query = jnp.dot(tokens, wq_full, preferred_element_type=jnp.float32).astype(jnp.bfloat16)
    keys = jnp.dot(flat, wk_full, preferred_element_type=jnp.float32).astype(jnp.bfloat16)
    values = jnp.dot(flat, wv_full, preferred_element_type=jnp.float32).astype(jnp.bfloat16)
    q_blocks = query.reshape(spans, CL, heads_here, HD)
    k_blocks = keys.reshape(spans, 2 * nlen, heads_here, HD)
    v_blocks = values.reshape(spans, 2 * nlen, heads_here, HD)
    scores = (
        jnp.einsum("cqhe,ckhe->chqk", q_blocks, k_blocks, preferred_element_type=jnp.float32)
        * scale
    )
    probs = jax.nn.softmax(scores, axis=-1)
    weights_b = probs.astype(jnp.bfloat16)
    mixed = (
        jnp.einsum("chqk,ckhe->cqhe", weights_b, v_blocks, preferred_element_type=jnp.float32)
        .astype(jnp.bfloat16)
        .reshape(tok_rows, local_width)
    )
    out_term = rounded(jnp.dot(mixed, wo_full, preferred_element_type=jnp.float32))
    cca_out = lax.psum_scatter(
        out_term.astype(jnp.bfloat16), "enc", scatter_dimension=1, tiled=True
    )
    d_mixed = jnp.dot(cotangent, wo_full.T, preferred_element_type=jnp.float32).astype(jnp.bfloat16)
    term_wo = rounded(jnp.dot(mixed.T, cotangent, preferred_element_type=jnp.float32))
    dm_blocks = d_mixed.reshape(spans, CL, heads_here, HD)
    dprob = jnp.einsum("cqhe,ckhe->chqk", dm_blocks, v_blocks, preferred_element_type=jnp.float32)
    dscore = (probs * (dprob - jnp.sum(dprob * probs, axis=-1, keepdims=True)) * scale).astype(
        jnp.bfloat16
    )
    d_query = (
        jnp.einsum("chqk,ckhe->cqhe", dscore, k_blocks, preferred_element_type=jnp.float32)
        .astype(jnp.bfloat16)
        .reshape(tok_rows, local_width)
    )
    d_keys = (
        jnp.einsum("chqk,cqhe->ckhe", dscore, q_blocks, preferred_element_type=jnp.float32)
        .astype(jnp.bfloat16)
        .reshape(count * nlen, local_width)
    )
    d_values = (
        jnp.einsum("chqk,cqhe->ckhe", weights_b, dm_blocks, preferred_element_type=jnp.float32)
        .astype(jnp.bfloat16)
        .reshape(count * nlen, local_width)
    )
    term_wq = rounded(jnp.dot(tokens.T, d_query, preferred_element_type=jnp.float32))
    term_wk = rounded(jnp.dot(flat.T, d_keys, preferred_element_type=jnp.float32))
    term_wv = rounded(jnp.dot(flat.T, d_values, preferred_element_type=jnp.float32))
    grad_wq, grad_wk, grad_wv, grad_wo = (
        lax.psum_scatter(
            term_wq.astype(jnp.bfloat16), "dp", scatter_dimension=0, tiled=True
        ).astype(jnp.float32),
        lax.psum_scatter(
            term_wk.astype(jnp.bfloat16), "dp", scatter_dimension=0, tiled=True
        ).astype(jnp.float32),
        lax.psum_scatter(
            term_wv.astype(jnp.bfloat16), "dp", scatter_dimension=0, tiled=True
        ).astype(jnp.float32),
        lax.psum_scatter(
            term_wo.astype(jnp.bfloat16), "dp", scatter_dimension=1, tiled=True
        ).astype(jnp.float32),
    )
    input_term = rounded(jnp.dot(d_query, wq_full.T, preferred_element_type=jnp.float32))
    grad_tokens = lax.psum_scatter(
        input_term.astype(jnp.bfloat16), "enc", scatter_dimension=1, tiled=True
    )
    return (
        cca_out,
        grad_tokens,
        grad_wq.astype(jnp.bfloat16),
        grad_wk.astype(jnp.bfloat16),
        grad_wv.astype(jnp.bfloat16),
        grad_wo.astype(jnp.bfloat16),
    )


def solution(mesh):
    placed = (
        P("dp", None),
        P(("dp", "enc"), None, None),
        P("dp", None),
        P("dp"),
        P("dp", "enc"),
        P("dp", "enc"),
        P("dp", "enc"),
        P("enc", "dp"),
        P("dp", None),
    )
    return jax.shard_map(
        body,
        mesh=mesh,
        in_specs=placed,
        out_specs=(
            P("dp", "enc"),
            P("dp", "enc"),
            P("dp", "enc"),
            P("dp", "enc"),
            P("dp", "enc"),
            P("enc", "dp"),
        ),
        check_vma=False,
    )
```

profile of v0, /device:TPU:0, one launch (start us, length us, event | category | flops | bytes accessed | tf_op | source)
XLA Modules:
  0.0 724.9 jit_solution(7754847366745258185)
XLA Ops:
  7.2 0.7 all-gather.10.cloned.1.call-update
  8.0 0.7 all-gather.14.cloned.1.call-update
  8.7 0.9 convert_reduce_fusion
  9.6 0.7 and_bitcast_fusion
  10.5 0.7 compare_convert_fusion
  11.1 0.8 multiply_reduce_fusion.1
  11.9 6.0 gather_fusion
  17.9 4.0 broadcast_select_fusion.1
  22.0 0.5 all-gather.12.cloned.1.call-update
  22.6 0.5 all-gather.8.cloned.1.call-update
  23.3 34.7 %all-gather.10.cloned.1.call-done = bf16[4096,256]{1,0:T(8,128)(2,1)} async-done(((bf16[256,256]{1,0:T(8,128)(2,1)}), bf16[4096,256]{1,0:T(8,128)(2,1)}) %all-gather.10.cloned.1.call-update) | async-done | bytes 2097168 | tf_op jit(solution)/shard_map/all_gather | solution.py:23
  57.9 2.3 convolution_convert_fusion.13
  60.3 46.9 %all-gather.14.cloned.1.call-done = bf16[256,4096]{1,0:T(8,128)(2,1)} async-done(((bf16[256,256]{1,0:T(8,128)(2,1)}), bf16[256,4096]{1,0:T(8,128)(2,1)}) %all-gather.14.cloned.1.call-update) | async-done | bytes 2097168 | tf_op jit(solution)/shard_map/all_gather | solution.py:26
  107.1 3.0 convolution_convert_fusion.12
  110.1 118.2 %all-gather.6.cloned.1.call-done = bf16[24,128,4096]{2,1,0:T(8,128)(2,1)} async-done(((bf16[3,128,4096]{2,1,0:T(8,128)(2,1)}), bf16[24,128,4096]{2,1,0:T(8,128)(2,1)}) %all-gather.6.cloned.1.call-update) | async-done | bytes 25165840 | tf_op jit(solution)/shard_map/all_gather | solution.py:36
  228.4 12.9 %gather_fusion.1 = bf16[8,128,4096]{2,1,0:T(8,128)(2,1)} fusion(bf16[24,128,4096]{2,1,0:T(8,128)(2,1)} %all-gather.6.cloned.1.call-done, s32[1024]{0:T(1024)S(1)} %pad_clamp_fusion), kind=kCustom, calls=%fused_computation.1 | custom fusion | bytes 16777248 | tf_op jit(solution)/shard_map/jit(_take)/gather | solution.py:40
  241.3 7.5 %bitcast_select_fusion = bf16[1024,4096]{1,0:T(8,128)(2,1)} fusion(bf16[8,128,4096]{2,1,0:T(8,128)(2,1)} %gather_fusion.1, pred[1024]{0:T(1024)(128)(4,1)S(1)} %broadcast_bitcast_fusion), kind=kLoop, calls=%fused_computation.4 | loop fusion | flops 4194304 | bytes 16778240 | tf_op jit(solution)/shard_map/jit(_take)/select_n | solution.py:40
  248.7 27.9 %all-gather.12.cloned.1.call-done = bf16[4096,256]{1,0:T(8,128)(2,1)} async-done(((bf16[256,256]{1,0:T(8,128)(2,1)}), bf16[4096,256]{1,0:T(8,128)(2,1)}) %all-gather.12.cloned.1.call-update) | async-done | bytes 2097168 | tf_op jit(solution)/shard_map/all_gather | solution.py:24
  276.6 6.3 convolution_convert_fusion.6
  283.1 0.3 convolution_multiply_fusion
  283.4 1.0 fusion.48
  284.4 38.8 %all-gather.8.cloned.1.call-done = bf16[4096,256]{1,0:T(8,128)(2,1)} async-done(((bf16[256,256]{1,0:T(8,128)(2,1)}), bf16[4096,256]{1,0:T(8,128)(2,1)}) %all-gather.8.cloned.1.call-update) | async-done | bytes 2097168 | tf_op jit(solution)/shard_map/all_gather | solution.py:25
  323.2 7.1 convolution_convert_fusion.7
  330.3 1.2 reshape.150
  331.5 1.1 fusion.21
  332.6 4.9 fusion.12
  337.5 1.0 copy.57
  338.5 2.1 fusion.2
  340.9 4.3 fusion.5
  345.2 0.4 copy.59
  345.6 7.5 %broadcast_select_fusion = bf16[8,128,4096]{2,1,0:T(8,128)(2,1)} fusion(bf16[8,128,4096]{2,1,0:T(8,128)(2,1)} %gather_fusion.1, pred[8]{0:T(512)(128)(4,1)S(1)} %get-tuple-element.30), kind=kLoop, calls=%fused_computation.5 | loop fusion | flops 4194304 | bytes 16777224 | tf_op jit(solution)/shard_map/jit(_take)/select_n | solution.py:40
  353.1 7.2 convolution_convert_fusion.1
  360.4 1.6 copy-done.3
  361.9 2.1 convolution_convert_fusion.4
  364.1 1.0 fusion.11
  365.2 0.4 copy-done.2
  365.6 2.1 convolution_convert_fusion.5
  367.7 1.1 fusion.6
  368.8 0.4 copy.61
  369.2 7.3 %convolution_convert_fusion = bf16[4096,256]{1,0:T(8,128)(2,1)} fusion(bf16[1024,4096]{1,0:T(8,128)(2,1)} %bitcast.73, bf16[128,8,2,128]{3,2,1,0:T(2,128)(2,1)S(1)} %bitcast.79), kind=kOutput, calls=%fused_computation.6 | convolution fusion | flops 2148532224 | bytes 11010048 | tf_op jit(solution)/shard_map/dot_general | solution.py:91
  376.6 3.8 convolution_convert_fusion.2
  380.4 34.2 %reduce-scatter.11.cloned.1.call-done = bf16[256,256]{0,1:T(8,128)(2,1)} async-done(((bf16[4096,256]{0,1:T(8,128)(2,1)}), bf16[256,256]{0,1:T(8,128)(2,1)}) %reduce-scatter.11.cloned.1.call-update) | async-done | bytes 131088 | tf_op jit(solution)/shard_map/reduce_scatter | solution.py:93
  414.6 1.7 copy.62
  416.3 76.1 %reduce-scatter.13.cloned.1.call-done = bf16[256,256]{1,0:T(8,128)(2,1)} async-done(((bf16[4096,256]{1,0:T(8,128)(2,1)}), bf16[256,256]{1,0:T(8,128)(2,1)}) %reduce-scatter.13.cloned.1.call-update) | async-done | bytes 131088 | tf_op jit(solution)/shard_map/reduce_scatter | solution.py:96
  492.3 35.8 %reduce-scatter.9.cloned.1.call-done = bf16[256,512]{1,0:T(8,128)(2,1)} async-done(((bf16[256,4096]{1,0:T(8,128)(2,1)}), bf16[256,512]{1,0:T(8,128)(2,1)}) %reduce-scatter.9.cloned.1.call-update) | async-done | bytes 262160 | tf_op jit(solution)/shard_map/reduce_scatter | solution.py:107
  528.1 35.5 %reduce-scatter.7.cloned.1.call-done = bf16[256,512]{1,0:T(8,128)(2,1)} async-done(((bf16[256,4096]{1,0:T(8,128)(2,1)}), bf16[256,512]{1,0:T(8,128)(2,1)}) %reduce-scatter.7.cloned.1.call-update) | async-done | bytes 262160 | tf_op jit(solution)/shard_map/reduce_scatter | solution.py:64
  563.6 77.0 %reduce-scatter.15.cloned.1.call-done = bf16[256,256]{1,0:T(8,128)(2,1)} async-done(((bf16[4096,256]{1,0:T(8,128)(2,1)}), bf16[256,256]{1,0:T(8,128)(2,1)}) %reduce-scatter.15.cloned.1.call-update) | async-done | bytes 131088 | tf_op jit(solution)/shard_map/reduce_scatter | solution.py:99
  640.6 77.8 %reduce-scatter.17.cloned.1.call-done = bf16[256,256]{1,0:T(8,128)(2,1)} async-done(((bf16[256,4096]{1,0:T(8,128)(2,1)}), bf16[256,256]{1,0:T(8,128)(2,1)}) %reduce-scatter.17.cloned.1.call-update) | async-done | bytes 131088 | tf_op jit(solution)/shard_map/reduce_scatter | solution.py:102
  (37 shorter events, 1.4 us)
Async XLA Ops:
  7.2 50.8 %copy-start = (bf16[256,4096]{1,0:T(8,128)(2,1)S(1)}, bf16[256,4096]{1,0:T(8,128)(2,1)}, u32[]{:S(2)}) copy-start(bf16[256,4096]{1,0:T(8,128)(2,1)} %param.9) | copy-start | bytes 6291460
  7.2 50.7 %all-gather.10.cloned.1.call-start = ((), (), s32[]{:S(2)}) async-start(), calls=%async_computation.8 | async-start | bytes 2228224 | tf_op jit(solution)/shard_map/all_gather | solution.py:23
  7.9 99.2 %all-gather.14.cloned.1.call-start = ((), (), s32[]{:S(2)}) async-start(), calls=%async_computation.10 | async-start | bytes 2228224 | tf_op jit(solution)/shard_map/all_gather | solution.py:26
  8.7 219.7 %all-gather.6.cloned.1.call-start = ((), (), s32[]{:S(2)}) async-start(), calls=%async_computation.6 | async-start | bytes 28311552 | tf_op jit(solution)/shard_map/all_gather | solution.py:36
  22.0 254.7 %all-gather.12.cloned.1.call-start = ((), (), s32[]{:S(2)}) async-start(), calls=%async_computation.9 | async-start | bytes 2228224 | tf_op jit(solution)/shard_map/all_gather | solution.py:24
  22.5 300.7 %all-gather.8.cloned.1.call-start = ((), (), s32[]{:S(2)}) async-start(), calls=%async_computation.7 | async-start | bytes 2228224 | tf_op jit(solution)/shard_map/all_gather | solution.py:25
  23.1 391.5 %reduce-scatter.11.cloned.1.call-start = ((), (), s32[]{:S(2)}) async-start(), calls=%async_computation.13 | async-start | bytes 2228224 | tf_op jit(solution)/shard_map/reduce_scatter | solution.py:93
  283.1 40.1 %copy-start.4 = (bf16[4,256,2,128]{3,2,1,0:T(2,128)(2,1)}, bf16[4,256,2,128]{3,2,1,0:T(2,128)(2,1)S(1)}, u32[]{:S(2)}) copy-start(bf16[4,256,2,128]{3,2,1,0:T(2,128)(2,1)S(1)} %reshape.152) | copy-start | bytes 1572868
  340.7 151.7 %reduce-scatter.13.cloned.1.call-start = ((), (), s32[]{:S(2)}) async-start(), calls=%async_computation.14 | async-start | bytes 2228224 | tf_op jit(solution)/shard_map/reduce_scatter | solution.py:96
  360.3 1.6 copy-start.3
  360.3 167.8 %reduce-scatter.9.cloned.1.call-start = ((), (), s32[]{:S(2)}) async-start(), calls=%async_computation.12 | async-start | bytes 2359296 | tf_op jit(solution)/shard_map/reduce_scatter | solution.py:107
  364.0 1.6 copy-start.2
  364.0 199.6 %reduce-scatter.7.cloned.1.call-start = ((), (), s32[]{:S(2)}) async-start(), calls=%async_computation.11 | async-start | bytes 2359296 | tf_op jit(solution)/shard_map/reduce_scatter | solution.py:64
  367.7 273.0 %reduce-scatter.15.cloned.1.call-start = ((), (), s32[]{:S(2)}) async-start(), calls=%async_computation.15 | async-start | bytes 2228224 | tf_op jit(solution)/shard_map/reduce_scatter | solution.py:99
  376.5 341.9 %reduce-scatter.17.cloned.1.call-start = ((), (), s32[]{:S(2)}) async-start(), calls=%async_computation.16 | async-start | bytes 2228224 | tf_op jit(solution)/shard_map/reduce_scatter | solution.py:102
  376.6 341.8 %copy-start.1 = (bf16[256,4096]{1,0:T(8,128)(2,1)S(1)}, bf16[256,4096]{1,0:T(8,128)(2,1)}, u32[]{:S(2)}) copy-start(bf16[256,4096]{1,0:T(8,128)(2,1)} %param.9) | copy-start | bytes 6291460
Sparse Core Ops, SparseCore 0:
  10.2 47.7 all-gather.9
  60.0 47.0 all-gather.13
  108.8 119.5 all-gather.5
  230.4 46.2 all-gather.11
  278.6 44.5 all-gather.7
  340.8 73.7 reduce-scatter.10
  418.8 73.4 reduce-scatter.12
  495.3 32.7 reduce-scatter.8
  531.1 32.4 reduce-scatter.6
  567.3 73.2 reduce-scatter.14
  644.8 73.5 reduce-scatter.16
where the time goes:
time: 726 us; the launch traced here: 725 us
  waiting for transfers between devices  605 us (83%)
  matrix products  55.8 us (8%)
  local copies, waits for them, and re-layouts  26 us (4%)
  other arithmetic  23.1 us (3%)
  between operations  14 us (2%)
    all_gather x1, waiting for transfers between devices, body(): arrived = lax.all_gather(outgoing, 'enc', axis=0, tiled=True)  118 us
    reduce_scatter x1, waiting for transfers between devices, body(): lax.psum_scatter(term_wo.astype(jnp.bfloat16), 'dp', scatter_dimension=1,...  77.8 us
    reduce_scatter x1, waiting for transfers between devices, body(): lax.psum_scatter(term_wv.astype(jnp.bfloat16), 'dp', scatter_dimension=0,...  77 us
    reduce_scatter x1, waiting for transfers between devices, body(): lax.psum_scatter(term_wk.astype(jnp.bfloat16), 'dp', scatter_dimension=0,...  76.1 us
    all_gather x1, waiting for transfers between devices, body(): lax.all_gather(wo, 'dp', axis=1, tiled=True)  46.9 us
    all_gather x1, waiting for transfers between devices, body(): lax.all_gather(wv, 'dp', axis=0, tiled=True)  38.8 us
    reduce_scatter x1, waiting for transfers between devices, body(): lax.psum_scatter(input_term.astype(jnp.bfloat16), 'enc', scatter_dimensio...  35.8 us
    reduce_scatter x1, waiting for transfers between devices, body(): lax.psum_scatter(out_term.astype(jnp.bfloat16), 'enc', scatter_dimension=...  35.5 us
  transfers between devices with their start and end apart: 11, of which 11 were waited for; matrix products, arithmetic and copies ran while one was open for 12% of the time, Pallas kernels for 0%

commit v1 on v0

v1 whole, which is shorter than its diff:
```python
import functools
import math

import jax
import jax.numpy as jnp
from jax import lax
from jax.experimental import pallas as pl
from jax.experimental.pallas import tpu as pltpu
from jax.sharding import PartitionSpec as P

ANY = pl.BlockSpec(memory_space=pl.ANY)
VMEM = pl.BlockSpec(memory_space=pltpu.VMEM)
SMEM = pl.BlockSpec(memory_space=pltpu.SMEM)
CAP = 3
STEPS = 9
TREES = 8
SEMS = 20
HD = 128


def place():
    dp = lax.axis_index("dp")
    enc = lax.axis_index("enc")
    return dp // 4, dp % 4, enc // 2, enc % 2


def around(value, by):
    return lax.rem(value + (4 + by), 4)


def remote(src, dst, send, recv, target):
    return pltpu.make_async_remote_copy(
        src_ref=src, dst_ref=dst, send_sem=send, recv_sem=recv,
        device_id=target, device_id_type=pl.DeviceIdType.MESH,
    )


def greet(peers):
    barrier = pltpu.get_barrier_semaphore()
    for peer in peers:
        pl.semaphore_signal(barrier, inc=1, device_id=peer, device_id_type=pl.DeviceIdType.MESH)
    pl.semaphore_wait(barrier, len(peers))


def gather_kernel(table, wq, wk, wv, wo, picked, weights, pool,
                  own, got, staged, tree_send, tree_recv, keep_sem,
                  ring_send, ring_recv, save_sem, pair_send, pair_recv):
    x, z, y, core = place()
    dp = x * 4 + z
    sources = (wk, wv, wq, wo)
    spots = (1, 2, 0, 3)

    def dp_at(axis, by):
        if axis == 0:
            return around(x, by) * 4 + z
        return x * 4 + around(z, by)

    def dp_of(first, o1, o2):
        if first == 0:
            return around(x, o1) * 4 + around(z, o2)
        return around(x, o2) * 4 + around(z, o1)

    def enc_at(by):
        return around(y, by) * 2 + core

    sibling = {"enc": y * 2 + 1 - core}
    greet([{"dp": dp_at(a, b)} for a in (0, 1) for b in (1, -1)]
          + [{"enc": enc_at(1)}, {"enc": enc_at(-1)}, sibling])

    sends = []

    def go(copy):
        copy.start()
        sends.append(copy)

    half = 128
    quarter = half // 2
    keeps = []
    for i in range(4):
        copy = pltpu.make_async_copy(sources[i], weights.at[spots[i], dp], keep_sem.at[i])
        copy.start()
        keeps.append(copy)

    def slot(t, j, part=None):
        w = t // 2
        r0 = (t % 2) * half
        if part is None:
            return weights.at[spots[w], j, pl.ds(r0, half)]
        return weights.at[spots[w], j, pl.ds(r0 + part * quarter, quarter)]

    def sem(t, k):
        return tree_send.at[t * SEMS + k], tree_recv.at[t * SEMS + k]

    def push(t, k, src, dst, axis, by):
        s, r = sem(t, k)
        go(remote(src, dst, s, r, {"dp": dp_at(axis, by)}))

    def landed(t, k, dst, axis, by):
        s, r = sem(t, k)
        remote(dst, dst, s, r, {"dp": dp_at(axis, by)}).wait_recv()

    def own_half(t):
        return sources[t // 2].at[pl.ds((t % 2) * half, half)]

    offsets = (0, -1, 1, 2)

    def tree_events(t):
        first = t % 2
        second = 1 - first
        me = dp

        def e0():
            push(t, 0, own_half(t), slot(t, me), first, 1)
            push(t, 1, own_half(t), slot(t, me), first, -1)

        def e0b():
            push(t, 4, own_half(t), slot(t, me), second, 1)
            push(t, 8, own_half(t), slot(t, me), second, -1)

        def e1():
            j = dp_of(first, -1, 0)
            landed(t, 0, slot(t, j), first, 1)
            push(t, 2, slot(t, j, 0), slot(t, j, 0), first, 1)
            push(t, 5, slot(t, j), slot(t, j), second, 1)
            push(t, 9, slot(t, j), slot(t, j), second, -1)

        def e2():
            j = dp_of(first, 1, 0)
            landed(t, 1, slot(t, j), first, -1)
            push(t, 3, slot(t, j, 1), slot(t, j, 1), first, -1)
            push(t, 6, slot(t, j), slot(t, j), second, 1)
            push(t, 10, slot(t, j), slot(t, j), second, -1)

        def e3():
            j = dp_of(first, 2, 0)
            landed(t, 2, slot(t, j, 0), first, 1)
            landed(t, 3, slot(t, j, 1), first, -1)
            push(t, 7, slot(t, j), slot(t, j), second, 1)
            push(t, 11, slot(t, j), slot(t, j), second, -1)

        def forward(k):
            def event():
                j = dp_of(first, offsets[k], -1)
                landed(t, 4 + k, slot(t, j), second, 1)
                push(t, 12 + k, slot(t, j, 0), slot(t, j, 0), second, 1)
                j = dp_of(first, offsets[k], 1)
                landed(t, 8 + k, slot(t, j), second, -1)
                push(t, 16 + k, slot(t, j, 1), slot(t, j, 1), second, -1)
            return event

        def finish(k):
            def event():
                j = dp_of(first, offsets[k], 2)
                landed(t, 12 + k, slot(t, j, 0), second, 1)
                landed(t, 16 + k, slot(t, j, 1), second, -1)
            return event

        return [e0, e0b, e1, e2, forward(0), e3, forward(1), forward(2), finish(0), forward(3),
                finish(1), finish(2), finish(3)]

    events = []
    per = [tree_events(t) for t in range(TREES)]
    for pair in range(TREES // 2):
        a, b = per[2 * pair], per[2 * pair + 1]
        for first_event, second_event in zip(a, b):
            events.append((pair * 1.0, first_event))
            events.append((pair * 1.0, second_event))
    per_pair = len(events) // (TREES // 2)
    SHIFT = 4
    keyed = []
    for i, (p, event) in enumerate(events):
        keyed.append(((i % per_pair) // 2 + SHIFT * p, p, i, event))
    keyed.sort(key=lambda item: item[:3])
    queue = [item[3] for item in keyed]
    total = len(queue)
    done = [0]

    def advance(upto):
        while done[0] < min(upto, total):
            queue[done[0]]()
            done[0] += 1

    mine = pl.ds(core * 64, 64)
    theirs = pl.ds((1 - core) * 64, 64)
    local = pltpu.make_async_copy(picked.at[:, mine], own.at[pl.ds(0, CAP)], keep_sem.at[4])
    local.start()
    mine_out = pltpu.make_async_copy(picked, pool.at[pl.ds(0, CAP)], keep_sem.at[5])
    mine_out.start()
    keeps.append(mine_out)
    swap = remote(picked.at[:, theirs], own.at[pl.ds(CAP, CAP)], pair_send.at[0], pair_recv.at[0], sibling)
    go(swap)
    advance(8)
    local.wait()
    swap.wait_recv()
    whole = remote(picked, pool.at[pl.ds(CAP, CAP)], pair_send.at[1], pair_recv.at[1], sibling)
    lag = table[0]
    saves = []
    for step in range(STEPS + 1):
        if step > 0:
            for way in (0, 1):
                ref = got.at[way, step - 1]
                remote(ref, ref, ring_send.at[way, step - 1], ring_recv.at[way, step - 1],
                       {"enc": enc_at(1 - 2 * way)}).wait_recv()
        if step < STEPS:
            take_own = step < table[1]
            index = table[2 + step]
            for way in (0, 1):
                rows = pl.ds(way * 32, 32)
                value = own[index, rows]
                for back in range(1, 7):
                    if step - back >= 0:
                        use = jnp.logical_and(jnp.logical_not(take_own), lag == back)
                        value = jnp.where(use, got[way, step - back], value)
                staged[way, step] = value
                go(remote(staged.at[way, step], got.at[way, step], ring_send.at[way, step],
                          ring_recv.at[way, step], {"enc": enc_at(1 - 2 * way)}))
        if step > 0:
            for way in (0, 1):
                dst = pool.at[2 * CAP + step - 1, pl.ds(core * 64 + way * 32, 32)]
                save = pltpu.make_async_copy(got.at[way, step - 1], dst, save_sem.at[way, step - 1])
                save.start()
                saves.append(save)
                go(remote(got.at[way, step - 1], dst, pair_send.at[2 + 2 * (step - 1) + way],
                          pair_recv.at[2 + 2 * (step - 1) + way], sibling))
        if step == 1:
            go(whole)
        advance(8 + (total - 8) * (step + 1) // (STEPS + 1))
    advance(total)
    whole.wait_recv()
    for step in range(STEPS):
        for way in (0, 1):
            dst = pool.at[2 * CAP + step, pl.ds((1 - core) * 64 + way * 32, 32)]
            remote(dst, dst, pair_send.at[2 + 2 * step + way], pair_recv.at[2 + 2 * step + way], sibling).wait_recv()
    for copy in keeps + saves:
        copy.wait()
    for copy in sends:
        copy.wait_send()


def gather_all(table, wq, wk, wv, wo, picked):
    return pl.pallas_call(
        gather_kernel,
        out_shape=(jax.ShapeDtypeStruct((4, 16, 256, 256), jnp.bfloat16),
                   jax.ShapeDtypeStruct((2 * CAP + STEPS, 128, 4096), jnp.bfloat16)),
        in_specs=[SMEM] + [ANY] * 5,
        out_specs=(ANY, ANY),
        scratch_shapes=[
            pltpu.VMEM((2 * CAP, 64, 4096), jnp.bfloat16),
            pltpu.VMEM((2, STEPS, 32, 4096), jnp.bfloat16),
            pltpu.VMEM((2, STEPS, 32, 4096), jnp.bfloat16),
            pltpu.SemaphoreType.DMA((TREES * SEMS,)),
            pltpu.SemaphoreType.DMA((TREES * SEMS,)),
            pltpu.SemaphoreType.DMA((6,)),
            pltpu.SemaphoreType.DMA((2, STEPS)),
            pltpu.SemaphoreType.DMA((2, STEPS)),
            pltpu.SemaphoreType.DMA((2, STEPS)),
            pltpu.SemaphoreType.DMA((2 + 2 * STEPS,)),
            pltpu.SemaphoreType.DMA((2 + 2 * STEPS,)),
        ],
        compiler_params=pltpu.CompilerParams(
            collective_id=0, has_side_effects=True, vmem_limit_bytes=48 * 1024 * 1024),
        name="gather_all",
    )(table, wq, wk, wv, wo, picked)


def routes(owners, enc):
    y, core = enc // 2, enc % 2
    count = owners.shape[0]
    places = jnp.arange(count, dtype=jnp.int32)
    chip = owners // 2
    earlier = places[None, :] < places[:, None]
    rank = jnp.sum(((owners[None, :] == owners[:, None]) & earlier).astype(jnp.int32), axis=1)
    chip_rank = jnp.sum(((chip[None, :] == chip[:, None]) & earlier).astype(jnp.int32), axis=1)
    held = jnp.sum((chip[None, :] == jnp.arange(4, dtype=jnp.int32)[:, None]).astype(jnp.int32), axis=1)
    lags = jnp.maximum(held, 1)
    here = chip == y
    n_here = jnp.sum(here.astype(jnp.int32))
    own_index = jnp.where(owners % 2 == core, rank, CAP + rank)
    steps = jnp.arange(STEPS, dtype=jnp.int32)
    match = here[None, :] & (chip_rank[None, :] == steps[:, None])
    order = jnp.sum(jnp.where(match, own_index[None, :], 0), axis=1)
    lag_here = jnp.maximum(n_here, 1)
    table = jnp.concatenate([lag_here[None], n_here[None], order]).astype(jnp.int32)
    spots = []
    for sign in (1, -1):
        hops = (y - chip) * sign % 4
        near = jnp.sum(jnp.where(jnp.arange(4)[None, :] == ((y - sign) % 4), lags[None, :], 0), axis=1)
        mid = jnp.sum(jnp.where(jnp.arange(4)[None, :] == ((y - 2 * sign) % 4), lags[None, :], 0), axis=1)
        spots.append(CAP + chip_rank + jnp.where(hops > 1, near, 0) + jnp.where(hops > 2, mid, 0))
    right = jnp.where(here, own_index, CAP + spots[0])
    left = jnp.where(here, own_index, CAP + spots[1])
    return table, right.astype(jnp.int32), left.astype(jnp.int32)


def pick_kernel(index, store, out):
    out[...] = store[...]


def pick(index, store):
    return pl.pallas_call(
        pick_kernel,
        out_shape=jax.ShapeDtypeStruct((CAP, 128, 4096), jnp.bfloat16),
        grid_spec=pltpu.PrefetchScalarGridSpec(
            num_scalar_prefetch=1,
            grid=(CAP, 2),
            in_specs=[pl.BlockSpec((1, 64, 4096), lambda i, j, index: (index[i], j, 0))],
            out_specs=pl.BlockSpec((1, 64, 4096), lambda i, j, index: (i, j, 0)),
        ),
        name="pick",
    )(index, store)


def my_picks(owners, rows, enc):
    mine = (owners == enc).astype(jnp.int32)
    order = jnp.cumsum(mine) - 1
    slot_ids = jnp.arange(CAP, dtype=jnp.int32)
    chosen = mine[None, :] * (order[None, :] == slot_ids[:, None]).astype(jnp.int32)
    return jnp.sum(chosen * rows[None, :], axis=1).astype(jnp.int32)


def add_to(dst, *parts):
    value = dst[...].astype(jnp.float32)
    for part in parts:
        value += part[...].astype(jnp.float32)
    dst[...] = value.astype(jnp.bfloat16)


def reduce_kernel(small, dkt, dvt, rows_in, tok_in, cot_in, weights,
                  cca, gtok, gq, gk, gv, go_out,
                  x, tok, cot, wq, wo, lhs, terms, outs, half1, full1, half2, full2,
                  pair_got, ring_half, ring_full,
                  load_sem, tree_send, tree_recv, out_send, out_recv):
    px, pz, py, core = place()

    def dp_at(axis, by):
        if axis == 0:
            return around(px, by) * 4 + pz
        return px * 4 + around(pz, by)

    def dp_of(first, o1, o2):
        if first == 0:
            return around(px, o1) * 4 + around(pz, o2)
        return around(px, o2) * 4 + around(pz, o1)

    def enc_at(by):
        return around(py, by) * 2 + core

    sibling = {"enc": py * 2 + 1 - core}
    loads = {}
    for i, (name, src, dst) in enumerate((
            ("small", small, lhs), ("cot", cot_in, cot), ("wo", weights.at[3], wo),
            ("x", rows_in, x), ("tok", tok_in, tok), ("wq", weights.at[0], wq))):
        loads[name] = pltpu.make_async_copy(src, dst, load_sem.at[i])
        loads[name].start()
    greet([{"dp": dp_at(a, b)} for a in (0, 1) for b in (1, -1)]
          + [{"enc": enc_at(1)}, {"enc": enc_at(-1)}, sibling])

    sends = []

    def go(copy):
        copy.start()
        sends.append(copy)

    def fill(w, left, right, chunk=256):
        def step(j, carry):
            cols = pl.ds(pl.multiple_of(j * 256, 256), 256)
            terms[w, j] = jnp.dot(left[...], right[:, cols], preferred_element_type=jnp.float32).astype(jnp.bfloat16)
            return carry
        lax.fori_loop(0, 16, step, 0)

    def fill_out(u, left, weight, flip):
        dims = (((1,), (1 if flip else 0,)), ((), ()))

        def step(j, carry):
            e = j // 2
            value = lax.dot_general(left[...], weight[j], dims, preferred_element_type=jnp.float32)
            cols = pl.ds(pl.multiple_of((j % 2) * 256, 256), 256)
            outs[u, e % 2, e // 2, :, cols] = value.astype(jnp.bfloat16)
            return carry
        lax.fori_loop(0, 16, step, 0)

    offsets = (2, -1, 1, 0)

    def tree(w, h):
        t = 2 * w + h
        first, second = h, 1 - h
        r0 = h * 128

        def block(o1, o2, part=None):
            j = dp_of(first, o1, o2)
            if part is None:
                return terms.at[w, j, pl.ds(r0, 128)]
            return terms.at[w, j, pl.ds(r0 + 64 * part, 64)]

        def push(k, src, dst, axis, by):
            go(remote(src, dst, tree_send.at[t * SEMS + k], tree_recv.at[t * SEMS + k], {"dp": dp_at(axis, by)}))

        def landed(k, dst, axis, by):
            remote(dst, dst, tree_send.at[t * SEMS + k], tree_recv.at[t * SEMS + k],
                   {"dp": dp_at(axis, by)}).wait_recv()

        def s1(k):
            def event():
                push(4 * k, block(offsets[k], 2, 0), half1.at[t, k, 0], second, 1)
                push(4 * k + 1, block(offsets[k], 2, 1), half1.at[t, k, 1], second, -1)
            return event

        def s2(k):
            def event():
                landed(4 * k, half1.at[t, k, 0], second, 1)
                add_to(block(offsets[k], 1, 0), half1.at[t, k, 0])
                push(4 * k + 2, block(offsets[k], 1), full1.at[t, k, 0], second, 1)
                landed(4 * k + 1, half1.at[t, k, 1], second, -1)
                add_to(block(offsets[k], -1, 1), half1.at[t, k, 1])
                push(4 * k + 3, block(offsets[k], -1), full1.at[t, k, 1], second, -1)
            return event

        def s3(k):
            def event():
                landed(4 * k + 2, full1.at[t, k, 0], second, 1)
                landed(4 * k + 3, full1.at[t, k, 1], second, -1)
                add_to(block(offsets[k], 0), full1.at[t, k, 0], full1.at[t, k, 1])
            return event

        def s4():
            push(16, block(2, 0, 0), half2.at[t, 0], first, 1)
            push(17, block(2, 0, 1), half2.at[t, 1], first, -1)

        def s5():
            landed(16, half2.at[t, 0], first, 1)
            add_to(block(1, 0, 0), half2.at[t, 0])
            push(18, block(1, 0), full2.at[t, 0], first, 1)
            landed(17, half2.at[t, 1], first, -1)
            add_to(block(-1, 0, 1), half2.at[t, 1])
            push(19, block(-1, 0), full2.at[t, 1], first, -1)

        def s6():
            landed(18, full2.at[t, 0], first, 1)
            landed(19, full2.at[t, 1], first, -1)
            value = (block(0, 0)[...].astype(jnp.float32) + full2[t, 0].astype(jnp.float32)
                     + full2[t, 1].astype(jnp.float32))
            if w == 3:
                go_out[pl.ds(r0, 128), :] = value.astype(jnp.bfloat16)
            else:
                (gq, gk, gv)[w][:, pl.ds(r0, 128)] = value.T.astype(jnp.bfloat16)

        return [s1(0), s1(1), s1(2), s1(3)], [
            s2(0), s2(1), s2(2), s2(3), s3(0), s4, s3(1), s3(2), s5, s3(3), s6]

    def output(u, final):
        def push(k, src, dst, target):
            go(remote(src, dst, out_send.at[u * 5 + k], out_recv.at[u * 5 + k], target))

        def landed(k, dst, target):
            remote(dst, dst, out_send.at[u * 5 + k], out_recv.at[u * 5 + k], target).wait_recv()

        ahead, behind = {"enc": enc_at(1)}, {"enc": enc_at(-1)}
        top, bottom = pl.ds(0, 128), pl.ds(128, 128)

        def block(by, part=None):
            if part is None:
                return outs.at[u, core, around(py, by)]
            return outs.at[u, core, around(py, by), (top, bottom)[part]]

        def p0():
            push(0, outs.at[u, 1 - core], pair_got.at[u], sibling)

        def p1():
            landed(0, pair_got.at[u], sibling)
            add_to(block(2), pair_got.at[u, around(py, 2)])
            push(1, block(2, 0), ring_half.at[u, 0], ahead)
            push(2, block(2, 1), ring_half.at[u, 1], behind)
            for by in (1, -1, 0):
                add_to(block(by), pair_got.at[u, around(py, by)])

        def p2():
            landed(1, ring_half.at[u, 0], ahead)
            add_to(block(1, 0), ring_half.at[u, 0])
            push(3, block(1), ring_full.at[u, 0], ahead)
            landed(2, ring_half.at[u, 1], behind)
            add_to(block(-1, 1), ring_half.at[u, 1])
            push(4, block(-1), ring_full.at[u, 1], behind)

        def p3():
            landed(3, ring_full.at[u, 0], ahead)
            landed(4, ring_full.at[u, 1], behind)
            value = (block(0)[...].astype(jnp.float32) + ring_full[u, 0].astype(jnp.float32)
                     + ring_full[u, 1].astype(jnp.float32))
            final[...] = value.astype(jnp.bfloat16)

        return [p0, p1, p2, p3]

    outs0, outs1 = output(0, cca), output(1, gtok)
    lists = {w: (tree(w, 0), tree(w, 1)) for w in (3, 2, 1, 0)}

    def begin(w):
        for k in range(4):
            lists[w][0][0][k]()
            lists[w][1][0][k]()

    def then(w, lo, hi):
        for k in range(lo, hi):
            lists[w][0][1][k]()
            lists[w][1][1][k]()

    loads["small"].wait()
    loads["cot"].wait()
    fill(3, lhs.at[2], cot)
    begin(3)
    loads["wo"].wait()
    fill_out(0, lhs.at[0], wo, False)
    outs0[0]()
    loads["x"].wait()
    fill(2, dvt, x)
    begin(2)
    then(3, 0, 4)
    fill(1, dkt, x)
    begin(1)
    outs0[1]()
    loads["tok"].wait()
    fill(0, lhs.at[3], tok)
    begin(0)
    loads["wq"].wait()
    fill_out(1, lhs.at[1], wq, True)
    outs1[0]()
    then(2, 0, 4)
    outs0[2]()
    outs1[1]()
    then(3, 4, 8)
    then(1, 0, 4)
    then(0, 0, 4)
    outs1[2]()
    outs0[3]()
    then(3, 8, 10)
    then(2, 4, 8)
    then(1, 4, 8)
    then(2, 8, 10)
    then(0, 4, 8)
    outs1[3]()
    then(1, 8, 10)
    then(3, 10, 11)
    then(0, 8, 10)
    then(2, 10, 11)
    then(1, 10, 11)
    then(0, 10, 11)
    for copy in sends:
        copy.wait_send()


def reduce_all(small, dkt, dvt, rows_in, tokens, cotangent, weights):
    bf = jnp.bfloat16
    return pl.pallas_call(
        reduce_kernel,
        out_shape=(jax.ShapeDtypeStruct((256, 512), bf), jax.ShapeDtypeStruct((256, 512), bf),
                   jax.ShapeDtypeStruct((256, 256), bf), jax.ShapeDtypeStruct((256, 256), bf),
                   jax.ShapeDtypeStruct((256, 256), bf), jax.ShapeDtypeStruct((256, 256), bf)),
        in_specs=[ANY, VMEM, VMEM, ANY, ANY, ANY, ANY],
        out_specs=(VMEM,) * 6,
        scratch_shapes=[
            pltpu.VMEM((1024, 4096), bf),
            pltpu.VMEM((256, 4096), bf),
            pltpu.VMEM((256, 4096), bf),
            pltpu.VMEM((16, 256, 256), bf),
            pltpu.VMEM((16, 256, 256), bf),
            pltpu.VMEM((4, 256, 256), bf),
            pltpu.VMEM((4, 16, 256, 256), bf),
            pltpu.VMEM((2, 2, 4, 256, 512), bf),
            pltpu.VMEM((TREES, 4, 2, 64, 256), bf),
            pltpu.VMEM((TREES, 4, 2, 128, 256), bf),
            pltpu.VMEM((TREES, 2, 64, 256), bf),
            pltpu.VMEM((TREES, 2, 128, 256), bf),
            pltpu.VMEM((2, 4, 256, 512), bf),
            pltpu.VMEM((2, 2, 128, 512), bf),
            pltpu.VMEM((2, 2, 256, 512), bf),
            pltpu.SemaphoreType.DMA((6,)),
            pltpu.SemaphoreType.DMA((TREES * SEMS,)),
            pltpu.SemaphoreType.DMA((TREES * SEMS,)),
            pltpu.SemaphoreType.DMA((10,)),
            pltpu.SemaphoreType.DMA((10,)),
        ],
        compiler_params=pltpu.CompilerParams(
            collective_id=1, has_side_effects=True, vmem_limit_bytes=56 * 1024 * 1024),
        name="reduce_all",
    )(small, dkt, dvt, rows_in, tokens, cotangent, weights)


def attend_kernel(right, left, pool, weights, tok_in, cot_in,
                  rows_out, small, dkt, dvt,
                  x, tok, cot, w, q, k, v, dm, load_sem, save_sem):
    scale = 1.0 / math.sqrt(HD)
    f32, bf = jnp.float32, jnp.bfloat16
    tok_load = pltpu.make_async_copy(tok_in, tok, load_sem.at[0])
    cot_load = pltpu.make_async_copy(cot_in, cot, load_sem.at[1])
    w_loads = [pltpu.make_async_copy(weights.at[i], w.at[i], load_sem.at[2 + i]) for i in range(4)]

    def part(n, p):
        index = (right, left)[p % 2][n]
        return pltpu.make_async_copy(pool.at[index, pl.ds(32 * p, 32)], x.at[n, pl.ds(32 * p, 32)],
                                     load_sem.at[6 + 4 * n + p])

    parts = [[part(n, p) for p in range(4)] for n in range(8)]
    w_loads[1].start()
    for n in range(2):
        for copy in parts[n]:
            copy.start()
    w_loads[2].start()
    for n in range(2, 8):
        for copy in parts[n]:
            copy.start()
    tok_load.start()
    w_loads[0].start()
    cot_load.start()
    w_loads[3].start()
    saves = []
    w_loads[1].wait()
    for c in range(4):
        for n in (2 * c, 2 * c + 1):
            for copy in parts[n]:
                copy.wait()
            save = pltpu.make_async_copy(x.at[n], rows_out.at[n], save_sem.at[n])
            save.start()
            saves.append(save)
        if c == 0:
            w_loads[2].wait()
        keyrows = x[2 * c:2 * c + 2].reshape(256, 4096)
        k[c] = jnp.dot(keyrows, w[1].reshape(4096, 256), preferred_element_type=f32).astype(bf)
        v[c] = jnp.dot(keyrows, w[2].reshape(4096, 256), preferred_element_type=f32).astype(bf)
    tok_load.wait()
    w_loads[0].wait()
    q[...] = jnp.dot(tok[...], w[0].reshape(4096, 256), preferred_element_type=f32).astype(bf)
    cot_load.wait()
    w_loads[3].wait()
    acc = jnp.zeros((256, 256), f32)
    nt = (((1,), (1,)), ((), ()))
    tn = (((0,), (0,)), ((), ()))
    for j in range(16):
        acc += lax.dot_general(cot[:, 256 * j:256 * j + 256], w[3, j], nt, preferred_element_type=f32)
    dm[...] = acc.astype(bf)
    for c in range(4):
        t = slice(64 * c, 64 * c + 64)
        for h in range(2):
            e = slice(128 * h, 128 * h + 128)
            qc, kc, vc, dc = q[t, e], k[c, :, e], v[c, :, e], dm[t, e]
            s = lax.dot_general(qc, kc, nt, preferred_element_type=f32) * scale
            p = jnp.exp(s - jnp.max(s, axis=-1, keepdims=True))
            p = p / jnp.sum(p, axis=-1, keepdims=True)
            pb = p.astype(bf)
            dp = lax.dot_general(dc, vc, nt, preferred_element_type=f32)
            ds = (p * (dp - jnp.sum(dp * p, axis=-1, keepdims=True)) * scale).astype(bf)
            small[0, t, e] = jnp.dot(pb, vc, preferred_element_type=f32).astype(bf)
            small[1, t, e] = jnp.dot(ds, kc, preferred_element_type=f32).astype(bf)
            dkt[e, 256 * c:256 * c + 256] = lax.dot_general(qc, ds, tn, preferred_element_type=f32).astype(bf)
            dvt[e, 256 * c:256 * c + 256] = lax.dot_general(dc, pb, tn, preferred_element_type=f32).astype(bf)
    small[2] = small[0].astype(f32).T.astype(bf)
    small[3] = small[1].astype(f32).T.astype(bf)
    for save in saves:
        save.wait()


def attend(right, left, pool, weights, tokens, cotangent):
    bf = jnp.bfloat16
    return pl.pallas_call(
        attend_kernel,
        out_shape=(jax.ShapeDtypeStruct((8, 128, 4096), bf), jax.ShapeDtypeStruct((4, 256, 256), bf),
                   jax.ShapeDtypeStruct((256, 1024), bf), jax.ShapeDtypeStruct((256, 1024), bf)),
        in_specs=[SMEM, SMEM, ANY, ANY, ANY, ANY],
        out_specs=(ANY, VMEM, VMEM, VMEM),
        scratch_shapes=[
            pltpu.VMEM((8, 128, 4096), bf),
            pltpu.VMEM((256, 4096), bf),
            pltpu.VMEM((256, 4096), bf),
            pltpu.VMEM((4, 16, 256, 256), bf),
            pltpu.VMEM((256, 256), bf),
            pltpu.VMEM((4, 256, 256), bf),
            pltpu.VMEM((4, 256, 256), bf),
            pltpu.VMEM((256, 256), bf),
            pltpu.SemaphoreType.DMA((38,)),
            pltpu.SemaphoreType.DMA((8,)),
        ],
        compiler_params=pltpu.CompilerParams(vmem_limit_bytes=48 * 1024 * 1024),
        name="attend",
    )(right, left, pool, weights, tokens, cotangent)


def body(tokens, store, holder, rows, wq, wk, wv, wo, cotangent):
    enc = lax.axis_index("enc")
    owners = holder[:, 0]
    table, right, left = routes(owners, enc)
    picked = pick(my_picks(owners, rows, enc), store)
    weights, pool = gather_all(table, wq, wk, wv, wo, picked)
    keyrows, small, dkt, dvt = attend(right, left, pool, weights, tokens, cotangent)
    return reduce_all(small, dkt, dvt, keyrows.reshape(1024, 4096), tokens, cotangent, weights)


def solution(mesh):
    placed = (
        P("dp", None), P(("dp", "enc"), None, None), P("dp", None), P("dp"),
        P("dp", "enc"), P("dp", "enc"), P("dp", "enc"), P("enc", "dp"), P("dp", None),
    )
    return jax.shard_map(
        body, mesh=mesh, in_specs=placed,
        out_specs=(P("dp", "enc"),) * 5 + (P("enc", "dp"),),
        check_vma=False,
    )
```

time: 726 us -> 200 us (0.28)
  waiting for transfers between devices: 605 us -> 0 us
  Pallas kernels: 0 us -> 172 us
  matrix products: 55.8 us -> 0 us
  between operations: 14 us -> 1.5 us
  other arithmetic: 23.1 us -> 10.7 us
  local copies, waits for them, and re-layouts: 26 us -> 15.5 us
    reduce_scatter x6 -> x0, waiting for transfers between devices: 336 us -> none  [the longest x1 77.8 us: body(): lax.psum_scatter(term_wo.astype(jnp.bfloat16), 'dp', scatter_dimension=1,...]
    all_gather x5 -> x0, waiting for transfers between devices: 266 us -> none  [the longest x1 118 us: body(): arrived = lax.all_gather(outgoing, 'enc', axis=0, tiled=True)]
    pallas_call x0 -> x4, Pallas kernels: none -> 172 us  [the longest x1 85.6 us: gather_all(): pl.pallas_call(gather_kernel, out_shape=(jax.ShapeDtypeStruct((4, 16, 256...]
    dot_general x16 -> x0, matrix products: 55.8 us -> none  [the longest x1 7.27 us: body(): jnp.dot(flat.T, d_values, preferred_element_type=jnp.float32)]
    gather x2 -> x0, local copies, waits for them, and re-layouts: 18.9 us -> none  [the longest x1 12.9 us: body(): neighbours = jnp.take(arrived, owners * CAP + rank, axis=0)]
    select_n x4 -> x2, other arithmetic: 18.9 us -> 3.28 us  [the longest x1 1.97 us: routes(): left = jnp.where(here, own_index, CAP + spots[1])]
    unnamed x11 -> x26, local copies, waits for them, and re-layouts: 3.65 us -> 15.5 us
  transfers between devices with their start and end apart: 11 -> 0, of which waited for: 11 -> 0; matrix products, arithmetic and copies ran while one was open for 12% -> 0% of each run, Pallas kernels for 0% -> 0%
where the time goes in v1:
time: 200 us
  Pallas kernels  172 us (86%)
  local copies, waits for them, and re-layouts  15.5 us (8%)
  other arithmetic  10.7 us (5%)
    pallas_call x1, Pallas kernels, gather_all(): pl.pallas_call(gather_kernel, out_shape=(jax.ShapeDtypeStruct((4, 16, 256...  85.6 us
    pallas_call x1, Pallas kernels, reduce_all(): pl.pallas_call(reduce_kernel, out_shape=(jax.ShapeDtypeStruct((256, 512),...  65.6 us
    unnamed x26, local copies, waits for them, and re-layouts  15.5 us
    pallas_call x1, Pallas kernels, attend(): pl.pallas_call(attend_kernel, out_shape=(jax.ShapeDtypeStruct((8, 128, 40...  14.8 us
    pallas_call x1, Pallas kernels, pick(): pl.pallas_call(pick_kernel, out_shape=jax.ShapeDtypeStruct((CAP, 128, 409...  6 us

profile of v1, /device:TPU:0, one launch (start us, length us, event | category | flops | bytes accessed | tf_op | source)
XLA Modules:
  0.0 199.7 jit_solution(10410367801875619309)
XLA Ops:
  0.6 0.0 copy-start.1
  0.6 0.0 copy-start.9
  0.7 0.0 copy-start.8
  0.7 0.0 copy-start.7
  0.7 0.0 copy-start.6
  0.8 0.8 compare_convert_fusion
  1.6 0.7 compare_convert_fusion.1
  2.2 0.2 reduce-window.8
  2.4 1.2 multiply_reduce_fusion.index
  3.7 0.7 fusion.13
  4.3 1.3 convert_reduce_fusion.3
  6.3 0.1 convert_reduce_fusion.2
  6.4 0.7 fusion.9
  7.1 0.9 convert_reduce_fusion
  8.0 2.0 add_select_fusion
  10.0 1.3 add_select_fusion.1.right
  11.3 0.1 select_reduce_fusion
  11.4 0.7 pad_add_fusion.table
  12.1 6.0 %pick.1.picked = bf16[3,128,4096]{2,1,0:T(8,128)(2,1)} custom-call(s32[3]{0:T(128)} %multiply_reduce_fusion.index, bf16[8,128,4096]{2,1,0:T(8,128)(2,1)} %store.1), custom_call_target="tpu_custom_call" | custom-call | tf_op jit(solution)/shard_map/pick/pallas_call | solution.py:300
  18.1 0.0 copy-done.9
  18.1 0.0 copy-done.8
  18.1 0.0 copy-done.7
  18.1 0.0 copy-done.6
  18.2 0.0 copy-start
  18.2 1.9 copy-done
  20.0 85.6 %gather_all.1 = (bf16[4,16,256,256]{3,2,1,0:T(8,128)(2,1)}, bf16[15,128,4096]{2,1,0:T(8,128)(2,1)}) custom-call(s32[11]{0:T(128)S(1)} %pad_add_fusion.table, bf16[256,256]{1,0:T(8,128)(2,1)S(1)} %copy-done.6, bf16[256,256]{1,0:T(8,128)(2,1)S(1)} %copy-done.7, bf16[256,256]{1,0:T(8,128)(2,1)S(1)} %copy-done.8, bf16[256,256]{1,0:T(8,128)(2,1)S(1)} %copy-done.9, ...), custom_call_target="tpu_custom_call" | custom-call | tf_op jit(solution)/shard_map/gather_all/pallas_call | solution.py:241
  105.7 0.0 copy-done.1
  105.7 0.0 copy-start.2
  105.7 1.6 copy-done.2
  107.3 14.8 %attend.1 = (bf16[8,128,4096]{2,1,0:T(8,128)(2,1)}, bf16[4,256,256]{2,1,0:T(8,128)(2,1)S(1)}, bf16[256,1024]{1,0:T(8,128)(2,1)S(1)}, bf16[256,1024]{1,0:T(8,128)(2,1)S(1)}) custom-call(s32[8]{0:T(128)S(1)} %add_select_fusion.1.right, s32[8]{0:T(128)S(1)} %get-tuple-element.24.left, bf16[15,128,4096]{2,1,0:T(8,128)(2,1)} %get-tuple-element.12.pool, ...), custom_call_target="tpu_custom_call" | custom-call | tf_op jit(solution)/shard_map/attend/pallas_call | solution.py:662
  122.1 0.0 copy-start.3
  122.1 0.8 copy-done.3
  122.9 0.0 copy-start.4
  122.9 0.8 copy-done.4
  123.7 0.0 copy-start.5
  123.7 0.8 copy-done.5
  124.5 65.6 %reduce_all.1 = (bf16[256,512]{1,0:T(8,128)(2,1)}, bf16[256,512]{1,0:T(8,128)(2,1)}, bf16[256,256]{1,0:T(8,128)(2,1)}, bf16[256,256]{1,0:T(8,128)(2,1)}, bf16[25...) custom-call(bf16[4,256,256]{2,1,0:T(8,128)(2,1)} %copy-done.3, bf16[256,1024]{1,0:T(8,128)(2,1)} %copy-done.4, ...), custom_call_target="tpu_custom_call" | custom-call | tf_op jit(solution)/shard_map/reduce_all/pallas_call | solution.py:552
  190.1 1.7 copy.21
  191.8 1.7 copy.22
  193.5 1.6 copy.23
  195.0 1.6 copy.24
  196.6 1.6 copy.25
  198.2 1.6 copy.26
  (2 shorter events, 0.0 us)
Async XLA Ops:
  0.6 105.1 %copy-start.1 = (bf16[256,4096]{1,0:T(8,128)(2,1)S(1)}, bf16[256,4096]{1,0:T(8,128)(2,1)}, u32[]{:S(2)}) copy-start(bf16[256,4096]{1,0:T(8,128)(2,1)} %tok_in.3) | copy-start | bytes 6291460
  0.6 17.5 %copy-start.9 = (bf16[256,256]{1,0:T(8,128)(2,1)S(1)}, bf16[256,256]{1,0:T(8,128)(2,1)}, u32[]{:S(2)}) copy-start(bf16[256,256]{1,0:T(8,128)(2,1)} %wo.1) | copy-start | bytes 393220
  0.7 17.5 %copy-start.8 = (bf16[256,256]{1,0:T(8,128)(2,1)S(1)}, bf16[256,256]{1,0:T(8,128)(2,1)}, u32[]{:S(2)}) copy-start(bf16[256,256]{1,0:T(8,128)(2,1)} %wv.1) | copy-start | bytes 393220
  0.7 17.5 %copy-start.7 = (bf16[256,256]{1,0:T(8,128)(2,1)S(1)}, bf16[256,256]{1,0:T(8,128)(2,1)}, u32[]{:S(2)}) copy-start(bf16[256,256]{1,0:T(8,128)(2,1)} %wk.1) | copy-start | bytes 393220
  0.7 17.5 %copy-start.6 = (bf16[256,256]{1,0:T(8,128)(2,1)S(1)}, bf16[256,256]{1,0:T(8,128)(2,1)}, u32[]{:S(2)}) copy-start(bf16[256,256]{1,0:T(8,128)(2,1)} %wq.1) | copy-start | bytes 393220
  18.2 1.9 copy-start
  105.7 1.6 copy-start.2
  122.1 0.8 copy-start.3
  122.9 0.8 copy-start.4
  123.7 0.8 copy-start.5

commit v2 on v1

v2 whole, which is shorter than its diff:
```python
import functools
import math

import jax
import jax.numpy as jnp
from jax import lax
from jax.experimental import pallas as pl
from jax.experimental.pallas import tpu as pltpu
from jax.sharding import PartitionSpec as P

ANY = pl.BlockSpec(memory_space=pl.ANY)
VMEM = pl.BlockSpec(memory_space=pltpu.VMEM)
SMEM = pl.BlockSpec(memory_space=pltpu.SMEM)
HD = 128
CAP = 3
STEPS = 9
SUBS = 2
SUB = 32 // SUBS
TREES = 8
SEMS = 20
STAGES = 9
NT = (((1,), (1,)), ((), ()))
TN = (((0,), (0,)), ((), ()))


def place():
    dp = lax.axis_index("dp")
    enc = lax.axis_index("enc")
    return dp // 4, dp % 4, enc // 2, enc % 2


def around(value, by):
    return lax.rem(value + (4 + by), 4)


def remote(src, dst, send, recv, target):
    return pltpu.make_async_remote_copy(
        src_ref=src, dst_ref=dst, send_sem=send, recv_sem=recv,
        device_id=target, device_id_type=pl.DeviceIdType.MESH,
    )


def greet(peers):
    barrier = pltpu.get_barrier_semaphore()
    for peer in peers:
        pl.semaphore_signal(barrier, inc=1, device_id=peer, device_id_type=pl.DeviceIdType.MESH)
    pl.semaphore_wait(barrier, len(peers))


def count_if(flag):
    return jnp.where(flag, 1, 0)


def routes(holder, rows, y, core):
    owner = [holder[n, 0] for n in range(8)]
    row = [rows[n] for n in range(8)]
    chip = [o // 2 for o in owner]
    here = [c == y for c in chip]
    rank, chip_rank = [], []
    for n in range(8):
        a, b = jnp.int32(0), jnp.int32(0)
        for m in range(n):
            a += count_if(owner[m] == owner[n])
            b += count_if(chip[m] == chip[n])
        rank.append(a)
        chip_rank.append(b)
    picks = []
    for k in range(CAP):
        value = jnp.int32(0)
        for n in range(8):
            value += jnp.where(jnp.logical_and(owner[n] == y * 2 + core, rank[n] == k), row[n], 0)
        picks.append(value)
    capped = [jnp.minimum(r, CAP - 1) for r in rank]
    own_index = [jnp.where(owner[n] % 2 == core, capped[n], CAP + capped[n]) for n in range(8)]
    order = []
    for t in range(2 * CAP):
        value = jnp.int32(0)
        for n in range(8):
            value += jnp.where(jnp.logical_and(here[n], chip_rank[n] == t), own_index[n], 0)
        order.append(value)

    def held(c):
        value = jnp.int32(0)
        for n in range(8):
            value += count_if(chip[n] == c)
        return value

    n_here = held(y)
    spots = []
    for sign in (1, -1):
        near = jnp.maximum(held(around(y, -sign)), 1)
        mid = jnp.maximum(held(around(y, -2 * sign)), 1)
        spot = []
        for n in range(8):
            hops = lax.rem((y - chip[n]) * sign + 4, 4)
            at = chip_rank[n] + jnp.where(hops > 1, near, 0) + jnp.where(hops > 2, mid, 0)
            spot.append(jnp.minimum(at, STEPS - 1))
        spots.append(spot)
    return picks, order, n_here, here, own_index, spots


def gather_kernel(holder, rows_in, store, wk, wv, wq, wo, tok_in, cot_in,
                  rows_out, small, dkt, dvt, wq_out, wo_out,
                  near, far, own_near, own_far, got, staged, weights, tok, cot,
                  kown_near, kown_far, kgot, vown_near, vown_far, vgot, q, k, v, dm,
                  load_sem, tree_send, tree_recv, ring_send, ring_recv, pair_send, pair_recv,
                  own_send, own_recv, save_sem):
    f32, bf = jnp.float32, jnp.bfloat16
    x, z, y, core = place()
    dp = x * 4 + z
    sources = (wk, wv, wq, wo)

    def dp_at(axis, by):
        if axis == 0:
            return around(x, by) * 4 + z
        return x * 4 + around(z, by)

    def dp_of(first, o1, o2):
        if first == 0:
            return around(x, o1) * 4 + around(z, o2)
        return around(x, o2) * 4 + around(z, o1)

    def enc_at(by):
        return around(y, by) * 2 + core

    sibling = {"enc": y * 2 + 1 - core}
    mine = pl.ds(core * 64, 64)
    theirs = pl.ds((1 - core) * 64, 64)
    load_far = pltpu.make_async_copy(store.at[:, theirs], far, load_sem.at[0])
    load_near = pltpu.make_async_copy(store.at[:, mine], near, load_sem.at[1])
    load_far.start()
    load_near.start()
    keeps = []
    for i in range(4):
        copy = pltpu.make_async_copy(sources[i], weights.at[i, dp], load_sem.at[2 + i])
        copy.start()
        keeps.append(copy)
    load_tok = pltpu.make_async_copy(tok_in, tok, load_sem.at[6])
    load_cot = pltpu.make_async_copy(cot_in, cot, load_sem.at[7])
    greet([{"dp": dp_at(a, b)} for a in (0, 1) for b in (1, -1)]
          + [{"enc": enc_at(1)}, {"enc": enc_at(-1)}, sibling])

    sends = []

    def go(copy):
        copy.start()
        sends.append(copy)

    half = 128
    quarter = half // 2

    def slot(t, j, part=None):
        r0 = (t % 2) * half
        if part is None:
            return weights.at[t // 2, j, pl.ds(r0, half)]
        return weights.at[t // 2, j, pl.ds(r0 + part * quarter, quarter)]

    def push(t, i, src, dst, axis, by):
        go(remote(src, dst, tree_send.at[t * SEMS + i], tree_recv.at[t * SEMS + i], {"dp": dp_at(axis, by)}))

    def landed(t, i, dst, axis, by):
        remote(dst, dst, tree_send.at[t * SEMS + i], tree_recv.at[t * SEMS + i], {"dp": dp_at(axis, by)}).wait_recv()

    offsets = (0, -1, 1, 2)

    def tree_events(t):
        first = t % 2
        second = 1 - first
        own_half = sources[t // 2].at[pl.ds((t % 2) * half, half)]

        def e0():
            push(t, 0, own_half, slot(t, dp), first, 1)
            push(t, 1, own_half, slot(t, dp), first, -1)

        def e0b():
            push(t, 4, own_half, slot(t, dp), second, 1)
            push(t, 8, own_half, slot(t, dp), second, -1)

        def e1():
            j = dp_of(first, -1, 0)
            landed(t, 0, slot(t, j), first, 1)
            push(t, 2, slot(t, j, 0), slot(t, j, 0), first, 1)
            push(t, 5, slot(t, j), slot(t, j), second, 1)
            push(t, 9, slot(t, j), slot(t, j), second, -1)

        def e2():
            j = dp_of(first, 1, 0)
            landed(t, 1, slot(t, j), first, -1)
            push(t, 3, slot(t, j, 1), slot(t, j, 1), first, -1)
            push(t, 6, slot(t, j), slot(t, j), second, 1)
            push(t, 10, slot(t, j), slot(t, j), second, -1)

        def e3():
            j = dp_of(first, 2, 0)
            landed(t, 2, slot(t, j, 0), first, 1)
            landed(t, 3, slot(t, j, 1), first, -1)
            push(t, 7, slot(t, j), slot(t, j), second, 1)
            push(t, 11, slot(t, j), slot(t, j), second, -1)

        def forward(i):
            def event():
                j = dp_of(first, offsets[i], -1)
                landed(t, 4 + i, slot(t, j), second, 1)
                push(t, 12 + i, slot(t, j, 0), slot(t, j, 0), second, 1)
                j = dp_of(first, offsets[i], 1)
                landed(t, 8 + i, slot(t, j), second, -1)
                push(t, 16 + i, slot(t, j, 1), slot(t, j, 1), second, -1)
            return event

        def finish(i):
            def event():
                j = dp_of(first, offsets[i], 2)
                landed(t, 12 + i, slot(t, j, 0), second, 1)
                landed(t, 16 + i, slot(t, j, 1), second, -1)
            return event

        return [e0, e0b, e1, e2, forward(0), e3, forward(1), forward(2), finish(0), forward(3),
                finish(1), finish(2), finish(3)]

    per = [tree_events(t) for t in range(TREES)]
    keyed = []
    for w in range(4):
        for i in range(13):
            for h in range(2):
                keyed.append((i + 4 * w, w, i, h))
    keyed.sort()
    queue = [per[2 * w + h][i] for _, w, i, h in keyed]
    ends = {w: keyed.index((12 + 4 * w, w, 12, 1)) + 1 for w in range(4)}
    total = len(queue)
    done = [0]

    def advance(upto):
        while done[0] < min(upto, total):
            queue[done[0]]()
            done[0] += 1

    advance(4)
    picks, order, n_here, here, own_index, spots = routes(holder, rows_in, y, core)
    lag = jnp.maximum(n_here, 1)
    load_far.wait()
    for i in range(CAP):
        own_far[i] = far[picks[i]]
    swap = remote(own_far.at[pl.ds(0, CAP)], own_near.at[pl.ds(CAP, CAP)], own_send.at[0], own_recv.at[0], sibling)
    go(swap)
    load_near.wait()
    for i in range(CAP):
        own_near[i] = near[picks[i]]
    load_tok.start()
    load_cot.start()
    advance(8)
    swap.wait_recv()
    swap_back = remote(own_near.at[pl.ds(0, CAP)], own_far.at[pl.ds(CAP, CAP)], own_send.at[1], own_recv.at[1], sibling)

    def lane(of, way, sub):
        return pl.ds(of * 64 + way * 32 + sub * SUB, SUB)

    def pair_wait(step):
        for way in (0, 1):
            for sub in range(SUBS):
                ref = got.at[step, lane(1 - core, way, sub)]
                remote(ref, ref, pair_send.at[step, way, sub], pair_recv.at[step, way, sub], sibling).wait_recv()

    def project(w, value):
        return jnp.dot(value, weights[w].reshape(4096, 256), preferred_element_type=f32).astype(bf)

    def kv_own():
        advance(ends[1])
        for copy in keeps[:2]:
            copy.wait()
        kown_near[...] = project(0, own_near[...].reshape(384, 4096)).reshape(6, 64, 256)
        vown_near[...] = project(1, own_near[...].reshape(384, 4096)).reshape(6, 64, 256)

    def kv_far():
        swap_back.wait_recv()
        kown_far[...] = project(0, own_far[...].reshape(384, 4096)).reshape(6, 64, 256)
        vown_far[...] = project(1, own_far[...].reshape(384, 4096)).reshape(6, 64, 256)

    def kv_got(lo, hi):
        def event():
            for step in range(lo, hi):
                pair_wait(step)
            m = (hi - lo) * 128
            value = got[lo:hi].reshape(m, 4096)
            kgot[lo:hi] = project(0, value).reshape(hi - lo, 128, 256)
            vgot[lo:hi] = project(1, value).reshape(hi - lo, 128, 256)
        return event

    def queries():
        advance(ends[2])
        keeps[2].wait()
        load_tok.wait()
        q[...] = project(2, tok[...])

    def upstream():
        advance(ends[3])
        keeps[3].wait()
        load_cot.wait()
        acc = jnp.zeros((256, 256), f32)
        for j in range(16):
            acc += lax.dot_general(cot[:, 256 * j:256 * j + 256], weights[3, j], NT, preferred_element_type=f32)
        dm[...] = acc.astype(bf)

    work = {10: kv_own, 11: kv_far, 12: kv_got(0, 2), 13: kv_got(2, 4), 15: queries, 16: kv_got(4, 6),
            18: upstream, 19: kv_got(6, 8)}
    for step in range(STEPS + 1):
        for sub in range(SUBS):
            for way in (0, 1):
                toward = {"enc": enc_at(1 - 2 * way)}
                if step > 0:
                    ref = got.at[step - 1, lane(core, way, sub)]
                    remote(ref, ref, ring_send.at[step - 1, way, sub], ring_recv.at[step - 1, way, sub], toward).wait_recv()
                if step < STEPS:
                    rows = pl.ds(way * 32 + sub * SUB, SUB)
                    value = own_near[order[min(step, 5)], rows]
                    for back in range(1, 7):
                        if step - back >= 0:
                            use = jnp.logical_and(n_here <= step, lag == back)
                            value = jnp.where(use, got[step - back, lane(core, way, sub)], value)
                    staged[step, way, sub] = value
                    go(remote(staged.at[step, way, sub], got.at[step, lane(core, way, sub)],
                              ring_send.at[step, way, sub], ring_recv.at[step, way, sub], toward))
                if step > 0:
                    ref = got.at[step - 1, lane(core, way, sub)]
                    go(remote(ref, ref, pair_send.at[step - 1, way, sub], pair_recv.at[step - 1, way, sub], sibling))
            if step == 1 and sub == 0:
                go(swap_back)
            s = SUBS * step + sub
            advance(8 + (total - 8) * (s + 1) // 17)
            if s in work:
                work[s]()
    advance(total)
    saves = [pltpu.make_async_copy(weights.at[2], wq_out, save_sem.at[0]),
             pltpu.make_async_copy(weights.at[3], wo_out, save_sem.at[1])]
    for copy in saves:
        copy.start()
    kv_got(8, 9)()

    for n in range(8):
        for way in (0, 1):
            part = pl.ds(way * 32, 32)
            at = spots[way][n]
            for dst, a, kb, vb, of in ((near, own_near, kown_near, vown_near, core),
                                       (far, own_far, kown_far, vown_far, 1 - core)):
                full = pl.ds(of * 64 + way * 32, 32)
                dst[n, part] = jnp.where(here[n], a[own_index[n], part], got[at, full])
                full_out = pl.ds((n % 2) * 128 + of * 64 + way * 32, 32)
                k[n // 2, full_out] = jnp.where(here[n], kb[own_index[n], part], kgot[at, full])
                v[n // 2, full_out] = jnp.where(here[n], vb[own_index[n], part], vgot[at, full])
    saves += [pltpu.make_async_copy(near, rows_out.at[:, mine], save_sem.at[2]),
              pltpu.make_async_copy(far, rows_out.at[:, theirs], save_sem.at[3])]
    saves[2].start()
    saves[3].start()

    scale = 1.0 / math.sqrt(HD)
    for c in range(4):
        t = slice(64 * c, 64 * c + 64)
        for h in range(2):
            e = slice(128 * h, 128 * h + 128)
            qc, kc, vc, dc = q[t, e], k[c, :, e], v[c, :, e], dm[t, e]
            s = lax.dot_general(qc, kc, NT, preferred_element_type=f32) * scale
            p = jnp.exp(s - jnp.max(s, axis=-1, keepdims=True))
            p = p / jnp.sum(p, axis=-1, keepdims=True)
            pb = p.astype(bf)
            dprob = lax.dot_general(dc, vc, NT, preferred_element_type=f32)
            ds = (p * (dprob - jnp.sum(dprob * p, axis=-1, keepdims=True)) * scale).astype(bf)
            small[0, t, e] = jnp.dot(pb, vc, preferred_element_type=f32).astype(bf)
            small[1, t, e] = jnp.dot(ds, kc, preferred_element_type=f32).astype(bf)
            dkt[e, 256 * c:256 * c + 256] = lax.dot_general(qc, ds, TN, preferred_element_type=f32).astype(bf)
            dvt[e, 256 * c:256 * c + 256] = lax.dot_general(dc, pb, TN, preferred_element_type=f32).astype(bf)
    small[2] = small[0].astype(f32).T.astype(bf)
    small[3] = small[1].astype(f32).T.astype(bf)
    for copy in saves:
        copy.wait()
    for copy in sends:
        copy.wait_send()


def gather_all(holder, rows, store, wk, wv, wq, wo, tokens, cotangent):
    bf = jnp.bfloat16
    dma = pltpu.SemaphoreType.DMA
    return pl.pallas_call(
        gather_kernel,
        out_shape=(jax.ShapeDtypeStruct((8, 128, 4096), bf), jax.ShapeDtypeStruct((4, 256, 256), bf),
                   jax.ShapeDtypeStruct((256, 1024), bf), jax.ShapeDtypeStruct((256, 1024), bf),
                   jax.ShapeDtypeStruct((16, 256, 256), bf), jax.ShapeDtypeStruct((16, 256, 256), bf)),
        in_specs=[SMEM, SMEM] + [ANY] * 7,
        out_specs=(ANY, VMEM, VMEM, VMEM, ANY, ANY),
        scratch_shapes=[
            pltpu.VMEM((8, 64, 4096), bf),
            pltpu.VMEM((8, 64, 4096), bf),
            pltpu.VMEM((2 * CAP, 64, 4096), bf),
            pltpu.VMEM((2 * CAP, 64, 4096), bf),
            pltpu.VMEM((STEPS, 128, 4096), bf),
            pltpu.VMEM((STAGES, 2, SUBS, SUB, 4096), bf),
            pltpu.VMEM((4, 16, 256, 256), bf),
            pltpu.VMEM((256, 4096), bf),
            pltpu.VMEM((256, 4096), bf),
            pltpu.VMEM((2 * CAP, 64, 256), bf),
            pltpu.VMEM((2 * CAP, 64, 256), bf),
            pltpu.VMEM((STEPS, 128, 256), bf),
            pltpu.VMEM((2 * CAP, 64, 256), bf),
            pltpu.VMEM((2 * CAP, 64, 256), bf),
            pltpu.VMEM((STEPS, 128, 256), bf),
            pltpu.VMEM((256, 256), bf),
            pltpu.VMEM((4, 256, 256), bf),
            pltpu.VMEM((4, 256, 256), bf),
            pltpu.VMEM((256, 256), bf),
            dma((8,)),
            dma((TREES * SEMS,)),
            dma((TREES * SEMS,)),
            dma((STEPS, 2, SUBS)),
            dma((STEPS, 2, SUBS)),
            dma((STEPS, 2, SUBS)),
            dma((STEPS, 2, SUBS)),
            dma((2,)),
            dma((2,)),
            dma((4,)),
        ],
        compiler_params=pltpu.CompilerParams(
            collective_id=0, has_side_effects=True, vmem_limit_bytes=60 * 1024 * 1024),
        name="gather_all",
    )(holder, rows, store, wk, wv, wq, wo, tokens, cotangent)


def add_to(dst, *parts):
    value = dst[...].astype(jnp.float32)
    for part in parts:
        value += part[...].astype(jnp.float32)
    dst[...] = value.astype(jnp.bfloat16)


def reduce_kernel(small, dkt_in, dvt_in, rows_in, tok_in, cot_in, wq_in, wo_in,
                  wide, square,
                  x, tok, cot, wq, wo, lhs, dkt, dvt, terms, outs, half1, full1, half2, full2,
                  pair_got, ring_half, ring_full,
                  load_sem, tree_send, tree_recv, out_send, out_recv):
    px, pz, py, core = place()

    def dp_at(axis, by):
        if axis == 0:
            return around(px, by) * 4 + pz
        return px * 4 + around(pz, by)

    def dp_of(first, o1, o2):
        if first == 0:
            return around(px, o1) * 4 + around(pz, o2)
        return around(px, o2) * 4 + around(pz, o1)

    def enc_at(by):
        return around(py, by) * 2 + core

    sibling = {"enc": py * 2 + 1 - core}
    loads = {}
    for i, (name, src, dst) in enumerate((
            ("small", small, lhs), ("cot", cot_in, cot), ("wo", wo_in, wo), ("dvt", dvt_in, dvt),
            ("x", rows_in, x), ("dkt", dkt_in, dkt), ("tok", tok_in, tok), ("wq", wq_in, wq))):
        loads[name] = pltpu.make_async_copy(src, dst, load_sem.at[i])
        loads[name].start()
    greet([{"dp": dp_at(a, b)} for a in (0, 1) for b in (1, -1)]
          + [{"enc": enc_at(1)}, {"enc": enc_at(-1)}, sibling])

    sends = []

    def go(copy):
        copy.start()
        sends.append(copy)

    def fill(w, left, right, chunk=256):
        def step(j, carry):
            cols = pl.ds(pl.multiple_of(j * 256, 256), 256)
            terms[w, j] = jnp.dot(left[...], right[:, cols], preferred_element_type=jnp.float32).astype(jnp.bfloat16)
            return carry
        lax.fori_loop(0, 16, step, 0)

    def fill_out(u, left, weight, flip):
        dims = (((1,), (1 if flip else 0,)), ((), ()))

        def step(j, carry):
            e = j // 2
            value = lax.dot_general(left[...], weight[j], dims, preferred_element_type=jnp.float32)
            cols = pl.ds(pl.multiple_of((j % 2) * 256, 256), 256)
            outs[u, e % 2, e // 2, :, cols] = value.astype(jnp.bfloat16)
            return carry
        lax.fori_loop(0, 16, step, 0)

    offsets = (2, -1, 1, 0)

    def tree(w, h):
        t = 2 * w + h
        first, second = h, 1 - h
        r0 = h * 128

        def block(o1, o2, part=None):
            j = dp_of(first, o1, o2)
            if part is None:
                return terms.at[w, j, pl.ds(r0, 128)]
            return terms.at[w, j, pl.ds(r0 + 64 * part, 64)]

        def push(k, src, dst, axis, by):
            go(remote(src, dst, tree_send.at[t * SEMS + k], tree_recv.at[t * SEMS + k], {"dp": dp_at(axis, by)}))

        def landed(k, dst, axis, by):
            remote(dst, dst, tree_send.at[t * SEMS + k], tree_recv.at[t * SEMS + k],
                   {"dp": dp_at(axis, by)}).wait_recv()

        def s1(k):
            def event():
                push(4 * k, block(offsets[k], 2, 0), half1.at[t, k, 0], second, 1)
                push(4 * k + 1, block(offsets[k], 2, 1), half1.at[t, k, 1], second, -1)
            return event

        def s2(k):
            def event():
                landed(4 * k, half1.at[t, k, 0], second, 1)
                add_to(block(offsets[k], 1, 0), half1.at[t, k, 0])
                push(4 * k + 2, block(offsets[k], 1), full1.at[t, k, 0], second, 1)
                landed(4 * k + 1, half1.at[t, k, 1], second, -1)
                add_to(block(offsets[k], -1, 1), half1.at[t, k, 1])
                push(4 * k + 3, block(offsets[k], -1), full1.at[t, k, 1], second, -1)
            return event

        def s3(k):
            def event():
                landed(4 * k + 2, full1.at[t, k, 0], second, 1)
                landed(4 * k + 3, full1.at[t, k, 1], second, -1)
                add_to(block(offsets[k], 0), full1.at[t, k, 0], full1.at[t, k, 1])
            return event

        def s4():
            push(16, block(2, 0, 0), half2.at[t, 0], first, 1)
            push(17, block(2, 0, 1), half2.at[t, 1], first, -1)

        def s5():
            landed(16, half2.at[t, 0], first, 1)
            add_to(block(1, 0, 0), half2.at[t, 0])
            push(18, block(1, 0), full2.at[t, 0], first, 1)
            landed(17, half2.at[t, 1], first, -1)
            add_to(block(-1, 0, 1), half2.at[t, 1])
            push(19, block(-1, 0), full2.at[t, 1], first, -1)

        def s6():
            landed(18, full2.at[t, 0], first, 1)
            landed(19, full2.at[t, 1], first, -1)
            value = (block(0, 0)[...].astype(jnp.float32) + full2[t, 0].astype(jnp.float32)
                     + full2[t, 1].astype(jnp.float32))
            square[w, pl.ds(r0, 128), :] = value.astype(jnp.bfloat16)

        return [s1(0), s1(1), s1(2), s1(3)], [
            s2(0), s2(1), s2(2), s2(3), s3(0), s4, s3(1), s3(2), s5, s3(3), s6]

    def output(u, final):
        def push(k, src, dst, target):
            go(remote(src, dst, out_send.at[u * 5 + k], out_recv.at[u * 5 + k], target))

        def landed(k, dst, target):
            remote(dst, dst, out_send.at[u * 5 + k], out_recv.at[u * 5 + k], target).wait_recv()

        ahead, behind = {"enc": enc_at(1)}, {"enc": enc_at(-1)}
        top, bottom = pl.ds(0, 128), pl.ds(128, 128)

        def block(by, part=None):
            if part is None:
                return outs.at[u, core, around(py, by)]
            return outs.at[u, core, around(py, by), (top, bottom)[part]]

        def p0():
            push(0, outs.at[u, 1 - core], pair_got.at[u], sibling)

        def p1():
            landed(0, pair_got.at[u], sibling)
            add_to(block(2), pair_got.at[u, around(py, 2)])
            push(1, block(2, 0), ring_half.at[u, 0], ahead)
            push(2, block(2, 1), ring_half.at[u, 1], behind)
            for by in (1, -1, 0):
                add_to(block(by), pair_got.at[u, around(py, by)])

        def p2():
            landed(1, ring_half.at[u, 0], ahead)
            add_to(block(1, 0), ring_half.at[u, 0])
            push(3, block(1), ring_full.at[u, 0], ahead)
            landed(2, ring_half.at[u, 1], behind)
            add_to(block(-1, 1), ring_half.at[u, 1])
            push(4, block(-1), ring_full.at[u, 1], behind)

        def p3():
            landed(3, ring_full.at[u, 0], ahead)
            landed(4, ring_full.at[u, 1], behind)
            value = (block(0)[...].astype(jnp.float32) + ring_full[u, 0].astype(jnp.float32)
                     + ring_full[u, 1].astype(jnp.float32))
            final[...] = value.astype(jnp.bfloat16)

        return [p0, p1, p2, p3]

    outs0, outs1 = output(0, wide.at[0]), output(1, wide.at[1])
    lists = {w: (tree(w, 0), tree(w, 1)) for w in (3, 2, 1, 0)}

    def begin(w):
        for k in range(4):
            lists[w][0][0][k]()
            lists[w][1][0][k]()

    def then(w, lo, hi):
        for k in range(lo, hi):
            lists[w][0][1][k]()
            lists[w][1][1][k]()

    loads["small"].wait()
    loads["cot"].wait()
    fill(3, lhs.at[2], cot)
    begin(3)
    loads["wo"].wait()
    fill_out(0, lhs.at[0], wo, False)
    outs0[0]()
    loads["x"].wait()
    loads["dvt"].wait()
    fill(2, dvt, x)
    begin(2)
    then(3, 0, 4)
    loads["dkt"].wait()
    fill(1, dkt, x)
    begin(1)
    outs0[1]()
    loads["tok"].wait()
    fill(0, lhs.at[3], tok)
    begin(0)
    loads["wq"].wait()
    fill_out(1, lhs.at[1], wq, True)
    outs1[0]()
    then(2, 0, 4)
    outs0[2]()
    outs1[1]()
    then(3, 4, 8)
    then(1, 0, 4)
    then(0, 0, 4)
    outs1[2]()
    outs0[3]()
    then(3, 8, 10)
    then(2, 4, 8)
    then(1, 4, 8)
    then(2, 8, 10)
    then(0, 4, 8)
    outs1[3]()
    then(1, 8, 10)
    then(3, 10, 11)
    then(0, 8, 10)
    then(2, 10, 11)
    then(1, 10, 11)
    then(0, 10, 11)
    for copy in sends:
        copy.wait_send()


def reduce_all(small, dkt, dvt, rows_in, tokens, cotangent, wq, wo):
    bf = jnp.bfloat16
    return pl.pallas_call(
        reduce_kernel,
        out_shape=(jax.ShapeDtypeStruct((2, 256, 512), bf), jax.ShapeDtypeStruct((4, 256, 256), bf)),
        in_specs=[ANY] * 8,
        out_specs=(VMEM,) * 2,
        scratch_shapes=[
            pltpu.VMEM((1024, 4096), bf),
            pltpu.VMEM((256, 4096), bf),
            pltpu.VMEM((256, 4096), bf),
            pltpu.VMEM((16, 256, 256), bf),
            pltpu.VMEM((16, 256, 256), bf),
            pltpu.VMEM((4, 256, 256), bf),
            pltpu.VMEM((256, 1024), bf),
            pltpu.VMEM((256, 1024), bf),
            pltpu.VMEM((4, 16, 256, 256), bf),
            pltpu.VMEM((2, 2, 4, 256, 512), bf),
            pltpu.VMEM((TREES, 4, 2, 64, 256), bf),
            pltpu.VMEM((TREES, 4, 2, 128, 256), bf),
            pltpu.VMEM((TREES, 2, 64, 256), bf),
            pltpu.VMEM((TREES, 2, 128, 256), bf),
            pltpu.VMEM((2, 4, 256, 512), bf),
            pltpu.VMEM((2, 2, 128, 512), bf),
            pltpu.VMEM((2, 2, 256, 512), bf),
            pltpu.SemaphoreType.DMA((8,)),
            pltpu.SemaphoreType.DMA((TREES * SEMS,)),
            pltpu.SemaphoreType.DMA((TREES * SEMS,)),
            pltpu.SemaphoreType.DMA((10,)),
            pltpu.SemaphoreType.DMA((10,)),
        ],
        compiler_params=pltpu.CompilerParams(
            collective_id=1, has_side_effects=True, vmem_limit_bytes=56 * 1024 * 1024),
        name="reduce_all",
    )(small, dkt, dvt, rows_in, tokens, cotangent, wq, wo)


def finish_kernel(wide, square, cca, gtok, gq, gk, gv, go_out):
    cca[...] = wide[0]
    gtok[...] = wide[1]
    for w, out in ((0, gq), (1, gk), (2, gv)):
        out[...] = square[w].astype(jnp.float32).T.astype(jnp.bfloat16)
    go_out[...] = square[3]


def finish(wide, square):
    bf = jnp.bfloat16
    return pl.pallas_call(
        finish_kernel,
        out_shape=(jax.ShapeDtypeStruct((256, 512), bf),) * 2 + (jax.ShapeDtypeStruct((256, 256), bf),) * 4,
        in_specs=[VMEM] * 2,
        out_specs=(VMEM,) * 6,
        name="finish",
    )(wide, square)


def body(tokens, store, holder, rows, wq, wk, wv, wo, cotangent):
    keyrows, small, dkt, dvt, wq_all, wo_all = gather_all(holder, rows, store, wk, wv, wq, wo, tokens, cotangent)
    wide, square = reduce_all(small, dkt, dvt, keyrows.reshape(1024, 4096), tokens, cotangent, wq_all, wo_all)
    return finish(wide, square)


def solution(mesh):
    placed = (
        P("dp", None), P(("dp", "enc"), None, None), P("dp", None), P("dp"),
        P("dp", "enc"), P("dp", "enc"), P("dp", "enc"), P("enc", "dp"), P("dp", None),
    )
    return jax.shard_map(
        body, mesh=mesh, in_specs=placed,
        out_specs=(P("dp", "enc"),) * 5 + (P("enc", "dp"),),
        check_vma=False,
    )
```

time: 200 us -> 149 us (0.74)
  Pallas kernels: 172 us -> 147 us
  local copies, waits for them, and re-layouts: 15.5 us -> 1.32 us
  other arithmetic: 10.7 us -> 0 us
    pallas_call x4 -> x3, Pallas kernels: 172 us -> 147 us  [the longest x1 81.5 us: gather_all(): pl.pallas_call(gather_kernel, out_shape=(jax.ShapeDtypeStruct((8, 128, 40...]
    unnamed x26 -> x1, local copies, waits for them, and re-layouts: 15.5 us -> 1.32 us
    reduce_sum x6 -> x0, other arithmetic: 4.37 us -> none  [the longest x1 1.3 us: routes(): n_here = jnp.sum(here.astype(jnp.int32))]
    select_n x2 -> x0, other arithmetic: 3.28 us -> none  [the longest x1 1.97 us: routes(): left = jnp.where(here, own_index, CAP + spots[1])]
where the time goes in v2:
time: 149 us
  Pallas kernels  147 us (99%)
    pallas_call x1, Pallas kernels, gather_all(): pl.pallas_call(gather_kernel, out_shape=(jax.ShapeDtypeStruct((8, 128, 40...  81.5 us
    pallas_call x1, Pallas kernels, reduce_all(): pl.pallas_call(reduce_kernel, out_shape=(jax.ShapeDtypeStruct((2, 256, 51...  62.9 us

profile of v2, /device:TPU:0, one launch (start us, length us, event | category | flops | bytes accessed | tf_op | source)
XLA Modules:
  0.0 148.6 jit_solution(6351786686444347191)
XLA Ops:
  0.6 1.3 copy.15.holder
  2.0 81.5 %gather_all.1 = (bf16[8,128,4096]{2,1,0:T(8,128)(2,1)}, bf16[4,256,256]{2,1,0:T(8,128)(2,1)}, bf16[256,1024]{1,0:T(8,128)(2,1)}, bf16[256,1024]{1,0:T(8,128)(2,1...) custom-call(s32[8,1]{1,0:T(8,128)} %copy.15.holder, s32[8]{0:T(128)} %rows_in.1, ...), custom_call_target="tpu_custom_call" | custom-call | tf_op jit(solution)/shard_map/gather_all/pallas_call | solution.py:381
  83.5 62.9 %reduce_all.1 = (bf16[2,256,512]{2,1,0:T(8,128)(2,1)}, bf16[4,256,256]{2,1,0:T(8,128)(2,1)}) custom-call(bf16[4,256,256]{2,1,0:T(8,128)(2,1)} %get-tuple-element.14.small, bf16[256,1024]{1,0:T(8,128)(2,1)} %get-tuple-element.15.dkt_in, bf16[256,1024]{1,0:T(8,128)(2,1)} %get-tuple-element.16.dvt_in, bf16[1024,4096]{1,0:T(8,128)(2,1)} %bitcast.1, ...), custom_call_target="tpu_custom_call" | custom-call | tf_op jit(solution)/shard_map/reduce_all/pallas_call | solution.py:655
  146.3 2.3 %finish.1 = (bf16[256,512]{1,0:T(8,128)(2,1)}, bf16[256,512]{1,0:T(8,128)(2,1)}, bf16[256,256]{1,0:T(8,128)(2,1)}, bf16[256,256]{1,0:T(8,128)(2,1)}, bf16[256,256]{1,0:T(8,128)(2,1)}, /*index=5*/bf16[256,256]{1,0:T(8,128)(2,1)}) custom-call(bf16[2,256,512]{2,1,0:T(8,128)(2,1)} %get-tuple-element.20.wide, bf16[4,256,256]{2,1,0:T(8,128)(2,1)} %get-tuple-element.21.square), custom_call_target="tpu_custom_call" | custom-call | tf_op jit(solution)/shard_map/finish/pallas_call | solution.py:700

commit v3 on v0

v3 whole, which is shorter than its diff:
```python
import functools
import math

import jax
import jax.numpy as jnp
from jax import lax
from jax.experimental import pallas as pl
from jax.experimental.pallas import tpu as pltpu
from jax.sharding import PartitionSpec as P

ANY = pl.BlockSpec(memory_space=pl.ANY)
VMEM = pl.BlockSpec(memory_space=pltpu.VMEM)
SMEM = pl.BlockSpec(memory_space=pltpu.SMEM)
HD = 128
CAP = 3
UNITS = 18
STAGES = 6
TREE_SPAN = 18
TREES = 8
SUM_SEMS = 10
TREE_SEMS = 7
NT = (((1,), (1,)), ((), ()))
TN = (((0,), (0,)), ((), ()))


def place():
    dp = lax.axis_index("dp")
    enc = lax.axis_index("enc")
    return dp // 4, dp % 4, enc // 2, enc % 2


def around(value, by):
    return lax.rem(value + (4 + by), 4)


def remote(src, dst, send, recv, target):
    return pltpu.make_async_remote_copy(
        src_ref=src, dst_ref=dst, send_sem=send, recv_sem=recv,
        device_id=target, device_id_type=pl.DeviceIdType.MESH,
    )


def count_if(flag):
    return jnp.where(flag, 1, 0)


def routes(holder, rows, y, core):
    owner = [holder[n, 0] for n in range(8)]
    row = [rows[n] for n in range(8)]
    chip = [o // 2 for o in owner]
    here = [c == y for c in chip]
    rank, chip_rank = [], []
    for n in range(8):
        a, b = jnp.int32(0), jnp.int32(0)
        for m in range(n):
            a += count_if(owner[m] == owner[n])
            b += count_if(chip[m] == chip[n])
        rank.append(a)
        chip_rank.append(b)
    picks = []
    for k in range(CAP):
        value = jnp.int32(0)
        for n in range(8):
            value += jnp.where(jnp.logical_and(owner[n] == y * 2 + core, rank[n] == k), row[n], 0)
        picks.append(value)
    capped = [jnp.minimum(r, CAP - 1) for r in rank]
    own_index = [jnp.where(owner[n] % 2 == core, capped[n], CAP + capped[n]) for n in range(8)]
    order = []
    for t in range(2 * CAP):
        value = jnp.int32(0)
        for n in range(8):
            value += jnp.where(jnp.logical_and(here[n], chip_rank[n] == t), own_index[n], 0)
        order.append(value)

    def held(c):
        value = jnp.int32(0)
        for n in range(8):
            value += count_if(chip[n] == c)
        return value

    n_here = held(y)
    spots = []
    for sign in (1, -1):
        near = 2 * jnp.maximum(held(around(y, -sign)), 1)
        mid = 2 * jnp.maximum(held(around(y, -2 * sign)), 1)
        spot = []
        for n in range(8):
            hops = lax.rem((y - chip[n]) * sign + 4, 4)
            at = 2 * chip_rank[n] + jnp.where(hops > 1, near, 0) + jnp.where(hops > 2, mid, 0)
            spot.append(jnp.minimum(at, UNITS - 2))
        spots.append(spot)
    return picks, order, n_here, here, own_index, spots


def add_to(dst, *parts):
    value = dst[...].astype(jnp.float32)
    for part in parts:
        value += part[...].astype(jnp.float32)
    dst[...] = value.astype(jnp.bfloat16)


def layer_kernel(holder, rows_in, store, wk, wv, wq, wo, tok_in, cot_in,
                 wide, square,
                 x, own_first, own_second, own_far, got, staged, weights, tok, cot,
                 kown_near, kown_far, kgot, vown_near, vown_far, vgot, q, k, v, dm, probs, small, dkt, dvt,
                 outs, half_a, full_a, half_b, full_b, half2_a, full2_a, half2_b, full2_b,
                 pair_got, ring_half, ring_full,
                 load_sem, tree_send, tree_recv, ring_send, ring_recv, pair_send, pair_recv,
                 own_send, own_recv, sum_send, sum_recv, out_send, out_recv):
    f32, bf = jnp.float32, jnp.bfloat16
    px, pz, y, core = place()
    dp = px * 4 + pz
    sources = (wk, wv, wq, wo)
    own_near = (own_first, own_second)

    def dp_at(axis, by):
        if axis == 0:
            return around(px, by) * 4 + pz
        return px * 4 + around(pz, by)

    def dp_of(first, o1, o2):
        if first == 0:
            return around(px, o1) * 4 + around(pz, o2)
        return around(px, o2) * 4 + around(pz, o1)

    def enc_at(by):
        return around(y, by) * 2 + core

    sibling = {"enc": y * 2 + 1 - core}
    load_store = pltpu.make_async_copy(store, x, load_sem.at[0])
    load_store.start()
    keeps = []
    for i in range(4):
        copy = pltpu.make_async_copy(sources[i], weights.at[i, dp], load_sem.at[1 + i])
        copy.start()
        keeps.append(copy)
    load_tok = pltpu.make_async_copy(tok_in, tok, load_sem.at[5])
    load_cot = pltpu.make_async_copy(cot_in, cot, load_sem.at[6])

    barrier = pltpu.get_barrier_semaphore()
    peers = ([{"dp": dp_at(a, b)} for a in (0, 1) for b in (1, -1)]
             + [{"enc": enc_at(1)}, {"enc": enc_at(-1)}, sibling])
    for peer in peers:
        pl.semaphore_signal(barrier, inc=1, device_id=peer, device_id_type=pl.DeviceIdType.MESH)
    picks, order, n_here, here, own_index, spots = routes(holder, rows_in, y, core)
    lag = 2 * jnp.maximum(n_here, 1)
    load_store.wait()

    def lane(of, way, r):
        return pl.ds(of * 64 + way * 32 + r * 16, 16)

    for r in (0, 1):
        for i in range(CAP):
            for way in (0, 1):
                own_far[r, i, way] = x[picks[i], lane(1 - core, way, r)]
                own_near[r][i, way] = x[picks[i], lane(core, way, r)]
    pl.semaphore_wait(barrier, len(peers))

    def slot(w, j, part=None):
        if part is None:
            return weights.at[w, j]
        return weights.at[w, j, pl.ds(part * 128, 128)]

    def push(w, group, src, dst, axis, by):
        remote(src, dst, tree_send.at[w], tree_recv.at[w, group], {"dp": dp_at(axis, by)}).start()

    def landed(w, group, pieces):
        ref = weights.at[w, pl.ds(0, pieces)]
        remote(ref, ref, tree_send.at[w], tree_recv.at[w, group], {"dp": dp_at(0, 1)}).wait_recv()

    def tree_sent(w):
        ref = weights.at[w, pl.ds(0, 15)]
        remote(ref, ref, tree_send.at[w], tree_recv.at[w, 0], {"dp": dp_at(0, 1)}).wait_send()

    offsets = (0, -1, 1, 2)

    def tree_events(w):
        first = w % 2
        second = 1 - first
        own_block = sources[w]

        def spread(i, src, j):
            push(w, 2 + i, src, slot(w, j), second, 1)
            push(w, 2 + i, src, slot(w, j), second, -1)

        def e0():
            push(w, 0, own_block, slot(w, dp), first, 1)
            push(w, 0, own_block, slot(w, dp), first, -1)

        def e1():
            spread(0, own_block, dp)

        def e2():
            landed(w, 0, 2)
            behind, ahead = dp_of(first, -1, 0), dp_of(first, 1, 0)
            push(w, 1, slot(w, behind, 0), slot(w, behind, 0), first, 1)
            push(w, 1, slot(w, ahead, 1), slot(w, ahead, 1), first, -1)
            spread(1, slot(w, behind), behind)
            spread(2, slot(w, ahead), ahead)

        def e3():
            landed(w, 1, 1)
            j = dp_of(first, 2, 0)
            spread(3, slot(w, j), j)

        def forward(i):
            def event():
                landed(w, 2 + i, 2)
                j = dp_of(first, offsets[i], -1)
                push(w, 6, slot(w, j, 0), slot(w, j, 0), second, 1)
                j = dp_of(first, offsets[i], 1)
                push(w, 6, slot(w, j, 1), slot(w, j, 1), second, -1)
            return event

        def last():
            landed(w, 6, 4)

        return [e0, e1, e2, forward(0), e3, forward(1), forward(2), forward(3), last]

    per = [tree_events(w) for w in range(4)]
    queue = []
    ends = {}
    for pair in ((0, 1), (2, 3)):
        for i in range(9):
            for w in pair:
                queue.append((i + 6 * (w // 2), w, i))
    queue.sort()
    for w in range(4):
        ends[w] = queue.index((8 + 6 * (w // 2), w, 8)) + 1
    queue = [per[w][i] for _, w, i in queue]
    total = len(queue)
    done = [0]

    def advance(upto):
        while done[0] < min(upto, total):
            queue[done[0]]()
            done[0] += 1

    swaps = [remote(own_far.at[r, pl.ds(0, CAP)], own_near[r].at[pl.ds(CAP, CAP)], own_send.at[r], own_recv.at[r], sibling)
             for r in (0, 1)]
    backs = [remote(own_near[r].at[pl.ds(0, CAP)], own_far.at[r, pl.ds(CAP, CAP)], own_send.at[2 + r], own_recv.at[2 + r], sibling)
             for r in (0, 1)]
    swaps[0].start()
    advance(2)
    swaps[1].start()
    load_tok.start()
    load_cot.start()
    advance(4)

    groups = ((0, 4), (4, 8), (8, 12), (12, 15), (15, 18))
    group_of = [i for i, (lo, hi) in enumerate(groups) for _ in range(lo, hi)]

    def pair_wait(group):
        lo, hi = groups[group]
        ref = got.at[pl.ds(lo, hi - lo), pl.ds(2 * (1 - core), 2)]
        remote(ref, ref, pair_send, pair_recv.at[group], sibling).wait_recv()

    def project(w, value):
        return jnp.dot(value, weights[w].reshape(4096, 256), preferred_element_type=f32).astype(bf)

    def kv_near():
        advance(ends[1])
        for copy in keeps[:2]:
            copy.wait()
        for r in (0, 1):
            value = own_near[r][...].reshape(192, 4096)
            kown_near[r] = project(0, value).reshape(6, 2, 16, 256)
            vown_near[r] = project(1, value).reshape(6, 2, 16, 256)

    def kv_far():
        for copy in backs:
            copy.wait_recv()
        value = own_far[...].reshape(384, 4096)
        kown_far[...] = project(0, value).reshape(2, 6, 2, 16, 256)
        vown_far[...] = project(1, value).reshape(2, 6, 2, 16, 256)

    def kv_got(group):
        def event():
            lo, hi = groups[group]
            pair_wait(group)
            value = got[lo:hi].reshape((hi - lo) * 64, 4096)
            kgot[lo:hi] = project(0, value).reshape(hi - lo, 4, 16, 256)
            vgot[lo:hi] = project(1, value).reshape(hi - lo, 4, 16, 256)
        return event

    def queries():
        advance(ends[2])
        keeps[2].wait()
        load_tok.wait()
        q[...] = project(2, tok[...])

    def upstream():
        advance(ends[3])
        keeps[3].wait()
        load_cot.wait()
        acc = jnp.zeros((256, 256), f32)
        for j in range(16):
            acc += lax.dot_general(cot[:, 256 * j:256 * j + 256], weights[3, j], NT, preferred_element_type=f32)
        dm[...] = acc.astype(bf)

    def ring_ref(u):
        return got.at[u, pl.ds(2 * core, 2)]

    def staged_sent(u):
        ref = staged.at[u % STAGES]
        remote(ref, ref, ring_send.at[u % STAGES], ring_recv.at[u], sibling).wait_send()

    work = {11: kv_near, 12: kv_far, 13: kv_got(0), 14: kv_got(1), 15: queries, 16: kv_got(2),
            18: upstream, 19: kv_got(3)}
    for u in range(UNITS + 2):
        if u >= 2:
            remote(ring_ref(u - 2), ring_ref(u - 2), ring_send.at[0], ring_recv.at[u - 2], sibling).wait_recv()
        if u < UNITS:
            if u < 2:
                swaps[u].wait_recv()
            if u >= STAGES:
                staged_sent(u - STAGES)
            for way in (0, 1):
                value = own_near[u % 2][order[min(u // 2, 5)], way]
                for back in (2, 4, 6, 8, 10, 12):
                    if u - back >= 0:
                        use = jnp.logical_and(2 * n_here <= u, lag == back)
                        value = jnp.where(use, got[u - back, 2 * core + way], value)
                staged[u % STAGES, way] = value
                remote(staged.at[u % STAGES, way], got.at[u, 2 * core + way],
                       ring_send.at[u % STAGES], ring_recv.at[u], {"enc": enc_at(1 - 2 * way)}).start()
        if u >= 2:
            remote(ring_ref(u - 2), ring_ref(u - 2), pair_send, pair_recv.at[group_of[u - 2]], sibling).start()
        if u in (2, 3):
            backs[u - 2].start()
        advance(4 + (total - 4) * (u + 1) // TREE_SPAN)
        if u in work:
            work[u]()
    advance(total)
    kv_got(4)()

    def key_rows(n, way, r, of, own, pool):
        return jnp.where(here[n], own, pool[spots[way][n] + r, 2 * of + way])

    for n in range(8):
        for way in (0, 1):
            for r in (0, 1):
                at = pl.ds((n % 2) * 128 + core * 64 + way * 32 + r * 16, 16)
                k[n // 2, at] = key_rows(n, way, r, core, kown_near[r, own_index[n], way], kgot)
                v[n // 2, at] = key_rows(n, way, r, core, vown_near[r, own_index[n], way], vgot)
                at = pl.ds((n % 2) * 128 + (1 - core) * 64 + way * 32 + r * 16, 16)
                k[n // 2, at] = key_rows(n, way, r, 1 - core, kown_far[r, own_index[n], way], kgot)
                v[n // 2, at] = key_rows(n, way, r, 1 - core, vown_far[r, own_index[n], way], vgot)

    def order_rows():
        for n in range(8):
            for way in (0, 1):
                for r in (0, 1):
                    x[n, lane(core, way, r)] = key_rows(n, way, r, core, own_near[r][own_index[n], way], got)
                    x[n, lane(1 - core, way, r)] = key_rows(n, way, r, 1 - core, own_far[r, own_index[n], way], got)

    scale = 1.0 / math.sqrt(HD)
    pairs = [(c, h, slice(64 * c, 64 * c + 64), slice(128 * h, 128 * h + 128)) for c in range(4) for h in range(2)]
    for c, h, t, e in pairs:
        s = lax.dot_general(q[t, e], k[c, :, e], NT, preferred_element_type=f32) * scale
        p = jnp.exp(s - jnp.max(s, axis=-1, keepdims=True))
        p = p / jnp.sum(p, axis=-1, keepdims=True)
        probs[c, h] = p
        small[0, t, e] = jnp.dot(p.astype(bf), v[c, :, e], preferred_element_type=f32).astype(bf)
    small[2] = small[0].astype(f32).T.astype(bf)

    def backward():
        for c, h, t, e in pairs:
            p = probs[c, h]
            dprob = lax.dot_general(dm[t, e], v[c, :, e], NT, preferred_element_type=f32)
            ds = (p * (dprob - jnp.sum(dprob * p, axis=-1, keepdims=True)) * scale).astype(bf)
            small[1, t, e] = jnp.dot(ds, k[c, :, e], preferred_element_type=f32).astype(bf)
            dkt[e, 256 * c:256 * c + 256] = lax.dot_general(q[t, e], ds, TN, preferred_element_type=f32).astype(bf)
            dvt[e, 256 * c:256 * c + 256] = lax.dot_general(dm[t, e], p.astype(bf), TN, preferred_element_type=f32).astype(bf)
        small[3] = small[1].astype(f32).T.astype(bf)

    def fill_flat(place_of, left, right):
        def step(j, carry):
            cols = pl.ds(pl.multiple_of(j * 256, 256), 256)
            weights[place_of, j] = jnp.dot(left[...], right[:, cols], preferred_element_type=f32).astype(bf)
            return carry
        lax.fori_loop(0, 16, step, 0)

    def fill_rows(place_of, left):
        def step(j, carry):
            cols = pl.ds(pl.multiple_of(j * 256, 256), 256)
            value = jnp.dot(left[...], x[:, :, cols].reshape(1024, 256), preferred_element_type=f32).astype(bf)
            got[4 * place_of:4 * place_of + 4, :, :, cols] = value.reshape(4, 4, 16, 256)
            return carry
        lax.fori_loop(0, 16, step, 0)

    def fill_out(u, left, w, flip):
        dims = (((1,), (1 if flip else 0,)), ((), ()))

        def step(j, carry):
            e = j // 2
            value = lax.dot_general(left[...], weights[w, j], dims, preferred_element_type=f32)
            cols = pl.ds(pl.multiple_of((j % 2) * 256, 256), 256)
            outs[u, e % 2, e // 2, :, cols] = value.astype(bf)
            return carry
        lax.fori_loop(0, 16, step, 0)

    ranks = (2, -1, 1, 0)

    def sum_tree(w, h):
        t = 2 * w + h
        first, second = h, 1 - h
        flat = w in (0, 3)
        if flat:
            b = 2 * (w == 0) + h
            half1, full1, half2, full2 = half_a.at[b], full_a.at[b], half2_a.at[b], full2_a.at[b]
        else:
            b = 2 * (w == 1) + h
            half1, full1, half2, full2 = half_b.at[b], full_b.at[b], half2_b.at[b], full2_b.at[b]

        def block(o1, o2, part=None):
            j = dp_of(first, o1, o2)
            if flat:
                if part is None:
                    return weights.at[int(w == 0), j, pl.ds(128 * h, 128)]
                return weights.at[int(w == 0), j, pl.ds(128 * h + 64 * part, 64)]
            cols = pl.ds(pl.multiple_of(j * 256, 256), 256)
            if part is None:
                return got.at[pl.ds(2 * b, 2), :, :, cols]
            return got.at[2 * b + part, :, :, cols]

        def push(group, src, dst, axis, by):
            remote(src, dst, sum_send.at[t], sum_recv.at[t, group], {"dp": dp_at(axis, by)}).start()

        def landed(group, ref):
            remote(ref, ref, sum_send.at[t], sum_recv.at[t, group], {"dp": dp_at(0, 1)}).wait_recv()

        def s1(i):
            def event():
                push(i, block(ranks[i], 2, 0), half1.at[i, 0], second, 1)
                push(i, block(ranks[i], 2, 1), half1.at[i, 1], second, -1)
            return event

        def s2(i):
            def event():
                landed(i, half1.at[i])
                add_to(block(ranks[i], 1, 0), half1.at[i, 0])
                push(4 + i, block(ranks[i], 1), full1.at[i, 0], second, 1)
                add_to(block(ranks[i], -1, 1), half1.at[i, 1])
                push(4 + i, block(ranks[i], -1), full1.at[i, 1], second, -1)
            return event

        def s3(i):
            def event():
                landed(4 + i, full1.at[i])
                add_to(block(ranks[i], 0), full1.at[i, 0], full1.at[i, 1])
            return event

        def s4():
            push(8, block(2, 0, 0), half2.at[0], first, 1)
            push(8, block(2, 0, 1), half2.at[1], first, -1)

        def s5():
            landed(8, half2)
            add_to(block(1, 0, 0), half2.at[0])
            push(9, block(1, 0), full2.at[0], first, 1)
            add_to(block(-1, 0, 1), half2.at[1])
            push(9, block(-1, 0), full2.at[1], first, -1)

        def s6():
            landed(9, full2)
            value = block(0, 0)[...].astype(f32) + full2[0].astype(f32) + full2[1].astype(f32)
            square[w, pl.ds(128 * h, 128), :] = value.astype(bf).reshape(128, 256)

        return [s1(0), s1(1), s1(2), s1(3)], [
            s2(0), s2(1), s2(2), s2(3), s3(0), s4, s3(1), s3(2), s5, s3(3), s6]

    def output(u, final):
        def push(group, src, dst, target):
            remote(src, dst, out_send.at[u, group], out_recv.at[u, group], target).start()

        def landed(group, ref):
            remote(ref, ref, out_send.at[u, group], out_recv.at[u, group], sibling).wait_recv()

        ahead, behind = {"enc": enc_at(1)}, {"enc": enc_at(-1)}
        top, bottom = pl.ds(0, 128), pl.ds(128, 128)

        def block(by, part=None):
            if part is None:
                return outs.at[u, core, around(y, by)]
            return outs.at[u, core, around(y, by), (top, bottom)[part]]

        def p0():
            push(0, outs.at[u, 1 - core], pair_got.at[u], sibling)

        def p1():
            landed(0, pair_got.at[u])
            add_to(block(2), pair_got.at[u, around(y, 2)])
            push(1, block(2, 0), ring_half.at[u, 0], ahead)
            push(1, block(2, 1), ring_half.at[u, 1], behind)
            for by in (1, -1, 0):
                add_to(block(by), pair_got.at[u, around(y, by)])

        def p2():
            landed(1, ring_half.at[u])
            add_to(block(1, 0), ring_half.at[u, 0])
            push(2, block(1), ring_full.at[u, 0], ahead)
            add_to(block(-1, 1), ring_half.at[u, 1])
            push(2, block(-1), ring_full.at[u, 1], behind)

        def p3():
            landed(2, ring_full.at[u])
            value = (block(0)[...].astype(jnp.float32) + ring_full[u, 0].astype(jnp.float32)
                     + ring_full[u, 1].astype(jnp.float32))
            final[...] = value.astype(jnp.bfloat16)

        return [p0, p1, p2, p3]

    outs0, outs1 = output(0, wide.at[0]), output(1, wide.at[1])
    lists = {w: (sum_tree(w, 0), sum_tree(w, 1)) for w in (3, 2, 1, 0)}

    def begin(w):
        for k in range(4):
            lists[w][0][0][k]()
            lists[w][1][0][k]()

    def then(w, lo, hi):
        for k in range(lo, hi):
            lists[w][0][1][k]()
            lists[w][1][1][k]()

    for w in range(4):
        tree_sent(w)
    for u in range(UNITS - STAGES, UNITS):
        staged_sent(u)
    remote(got.at[:, pl.ds(0, 2)], got.at[:, pl.ds(0, 2)], pair_send, pair_recv.at[0], sibling).wait_send()
    for copy in swaps + backs:
        copy.wait_send()
    fill_flat(0, small.at[2], cot)
    begin(3)
    fill_out(0, small.at[0], 3, False)
    outs0[0]()
    backward()
    fill_flat(1, small.at[3], tok)
    begin(0)
    then(3, 0, 4)
    order_rows()
    fill_rows(0, dvt)
    begin(2)
    then(0, 0, 4)
    outs0[1]()
    fill_rows(1, dkt)
    begin(1)
    then(3, 4, 8)
    fill_out(1, small.at[1], 2, True)
    outs1[0]()
    then(2, 0, 4)
    outs0[2]()
    then(0, 4, 8)
    then(1, 0, 4)
    outs1[1]()
    then(3, 8, 10)
    outs0[3]()
    then(2, 4, 8)
    outs1[2]()
    then(0, 8, 10)
    then(1, 4, 8)
    then(3, 10, 11)
    then(2, 8, 10)
    outs1[3]()
    then(0, 10, 11)
    then(1, 8, 10)
    then(2, 10, 11)
    then(1, 10, 11)
    for t in range(TREES):
        ref = weights.at[3, pl.ds(0, 15), pl.ds(0, 128)]
        remote(ref, ref, sum_send.at[t], sum_recv.at[t, 0], sibling).wait_send()
    for u in (0, 1):
        for group, ref in enumerate((pair_got.at[u], ring_half.at[u], ring_full.at[u])):
            remote(ref, ref, out_send.at[u, group], out_recv.at[u, group], sibling).wait_send()


def layer(holder, rows, store, wk, wv, wq, wo, tokens, cotangent):
    bf = jnp.bfloat16
    dma = pltpu.SemaphoreType.DMA
    vm = pltpu.VMEM
    return pl.pallas_call(
        layer_kernel,
        out_shape=(jax.ShapeDtypeStruct((2, 256, 512), bf), jax.ShapeDtypeStruct((4, 256, 256), bf)),
        in_specs=[SMEM, SMEM] + [ANY] * 7,
        out_specs=(VMEM, VMEM),
        scratch_shapes=[
            vm((8, 128, 4096), bf),
            vm((2 * CAP, 2, 16, 4096), bf),
            vm((2 * CAP, 2, 16, 4096), bf),
            vm((2, 2 * CAP, 2, 16, 4096), bf),
            vm((UNITS, 4, 16, 4096), bf),
            vm((STAGES, 2, 16, 4096), bf),
            vm((4, 16, 256, 256), bf),
            vm((256, 4096), bf),
            vm((256, 4096), bf),
            vm((2, 2 * CAP, 2, 16, 256), bf),
            vm((2, 2 * CAP, 2, 16, 256), bf),
            vm((UNITS, 4, 16, 256), bf),
            vm((2, 2 * CAP, 2, 16, 256), bf),
            vm((2, 2 * CAP, 2, 16, 256), bf),
            vm((UNITS, 4, 16, 256), bf),
            vm((256, 256), bf),
            vm((4, 256, 256), bf),
            vm((4, 256, 256), bf),
            vm((256, 256), bf),
            vm((4, 2, 64, 256), jnp.float32),
            vm((4, 256, 256), bf),
            vm((256, 1024), bf),
            vm((256, 1024), bf),
            vm((2, 2, 4, 256, 512), bf),
            vm((4, 4, 2, 64, 256), bf),
            vm((4, 4, 2, 128, 256), bf),
            vm((4, 4, 2, 4, 16, 256), bf),
            vm((4, 4, 2, 2, 4, 16, 256), bf),
            vm((4, 2, 64, 256), bf),
            vm((4, 2, 128, 256), bf),
            vm((4, 2, 4, 16, 256), bf),
            vm((4, 2, 2, 4, 16, 256), bf),
            vm((2, 4, 256, 512), bf),
            vm((2, 2, 128, 512), bf),
            vm((2, 2, 256, 512), bf),
            dma((7,)),
            dma((4,)),
            dma((4, TREE_SEMS)),
            dma((STAGES,)),
            dma((UNITS,)),
            dma(()),
            dma((5,)),
            dma((4,)),
            dma((4,)),
            dma((TREES,)),
            dma((TREES, SUM_SEMS)),
            dma((2, 3)),
            dma((2, 3)),
        ],
        compiler_params=pltpu.CompilerParams(
            collective_id=0, has_side_effects=True, vmem_limit_bytes=62 * 1024 * 1024),
        name="layer",
    )(holder, rows, store, wk, wv, wq, wo, tokens, cotangent)


def finish_kernel(wide, square, cca, gtok, gq, gk, gv, go_out):
    cca[...] = wide[0]
    gtok[...] = wide[1]
    for w, out in ((0, gq), (1, gk), (2, gv)):
        out[...] = square[w].astype(jnp.float32).T.astype(jnp.bfloat16)
    go_out[...] = square[3]


def finish(wide, square):
    bf = jnp.bfloat16
    return pl.pallas_call(
        finish_kernel,
        out_shape=(jax.ShapeDtypeStruct((256, 512), bf),) * 2 + (jax.ShapeDtypeStruct((256, 256), bf),) * 4,
        in_specs=[VMEM] * 2,
        out_specs=(VMEM,) * 6,
        name="finish",
    )(wide, square)


def body(tokens, store, holder, rows, wq, wk, wv, wo, cotangent):
    return finish(*layer(holder, rows, store, wk, wv, wq, wo, tokens, cotangent))


def solution(mesh):
    placed = (
        P("dp", None), P(("dp", "enc"), None, None), P("dp", None), P("dp"),
        P("dp", "enc"), P("dp", "enc"), P("dp", "enc"), P("enc", "dp"), P("dp", None),
    )
    return jax.shard_map(
        body, mesh=mesh, in_specs=placed,
        out_specs=(P("dp", "enc"),) * 5 + (P("enc", "dp"),),
        check_vma=False,
    )
```

time: 726 us -> 136 us (0.19)
  waiting for transfers between devices: 605 us -> 0 us
  Pallas kernels: 0 us -> 134 us
  matrix products: 55.8 us -> 0 us
  local copies, waits for them, and re-layouts: 26 us -> 1.32 us
  other arithmetic: 23.1 us -> 0 us
  between operations: 14 us -> 0.64 us
    reduce_scatter x6 -> x0, waiting for transfers between devices: 336 us -> none  [the longest x1 77.8 us: body(): lax.psum_scatter(term_wo.astype(jnp.bfloat16), 'dp', scatter_dimension=1,...]
    all_gather x5 -> x0, waiting for transfers between devices: 266 us -> none  [the longest x1 118 us: body(): arrived = lax.all_gather(outgoing, 'enc', axis=0, tiled=True)]
    pallas_call x0 -> x2, Pallas kernels: none -> 134 us  [the longest x1 132 us: layer(): pl.pallas_call(layer_kernel, out_shape=(jax.ShapeDtypeStruct((2, 256, 512...]
    dot_general x16 -> x0, matrix products: 55.8 us -> none  [the longest x1 7.27 us: body(): jnp.dot(flat.T, d_values, preferred_element_type=jnp.float32)]
    select_n x4 -> x0, other arithmetic: 18.9 us -> none  [the longest x2 14.9 us: body(): neighbours = jnp.take(arrived, owners * CAP + rank, axis=0)]
    gather x2 -> x0, local copies, waits for them, and re-layouts: 18.9 us -> none  [the longest x1 12.9 us: body(): neighbours = jnp.take(arrived, owners * CAP + rank, axis=0)]
  transfers between devices with their start and end apart: 11 -> 0, of which waited for: 11 -> 0; matrix products, arithmetic and copies ran while one was open for 12% -> 0% of each run, Pallas kernels for 0% -> 0%
where the time goes in v3:
time: 136 us
  Pallas kernels  134 us (99%)
    pallas_call x1, Pallas kernels, layer(): pl.pallas_call(layer_kernel, out_shape=(jax.ShapeDtypeStruct((2, 256, 512...  132 us

profile of v3, /device:TPU:0, one launch (start us, length us, event | category | flops | bytes accessed | tf_op | source)
XLA Modules:
  0.0 135.8 jit_solution(5625244079491737697)
XLA Ops:
  0.6 1.3 copy.15.holder
  2.0 131.6 %layer.1 = (bf16[2,256,512]{2,1,0:T(8,128)(2,1)}, bf16[4,256,256]{2,1,0:T(8,128)(2,1)}) custom-call(s32[8,1]{1,0:T(8,128)} %copy.15.holder, s32[8]{0:T(128)} %rows_in.1, bf16[8,128,4096]{2,1,0:T(8,128)(2,1)} %store.1, bf16[256,256]{1,0:T(8,128)(2,1)} %wk.1, bf16[256,256]{1,0:T(8,128)(2,1)} %wv.1, bf16[256,256]{1,0:T(8,128)(2,1)} %wq.1, bf16[256,256]{1,0:T(8,128)(2,1)} %wo.1, ...), custom_call_target="tpu_custom_call" | custom-call | tf_op jit(solution)/shard_map/layer/pallas_call | solution.py:582
  133.5 2.3 %finish.1 = (bf16[256,512]{1,0:T(8,128)(2,1)}, bf16[256,512]{1,0:T(8,128)(2,1)}, bf16[256,256]{1,0:T(8,128)(2,1)}, bf16[256,256]{1,0:T(8,128)(2,1)}, bf16[256,256]{1,0:T(8,128)(2,1)}, /*index=5*/bf16[256,256]{1,0:T(8,128)(2,1)}) custom-call(bf16[2,256,512]{2,1,0:T(8,128)(2,1)} %get-tuple-element.8.wide, bf16[4,256,256]{2,1,0:T(8,128)(2,1)} %get-tuple-element.9.square), custom_call_target="tpu_custom_call" | custom-call | tf_op jit(solution)/shard_map/finish/pallas_call | solution.py:653

commit v4 on v3

--- a/solution.py
+++ b/solution.py
@@ -16,6 +16,7 @@
 UNITS = 18
 STAGES = 6
 TREE_SPAN = 18
+UNROLL = 1
 TREES = 8
 SUM_SEMS = 10
 TREE_SEMS = 7
@@ -45,7 +46,7 @@
 
 
 def routes(holder, rows, y, core):
-    owner = [holder[n, 0] for n in range(8)]
+    owner = [holder[n] for n in range(8)]
     row = [rows[n] for n in range(8)]
     chip = [o // 2 for o in owner]
     here = [c == y for c in chip]
@@ -102,7 +103,7 @@
 def layer_kernel(holder, rows_in, store, wk, wv, wq, wo, tok_in, cot_in,
                  wide, square,
                  x, own_first, own_second, own_far, got, staged, weights, tok, cot,
-                 kown_near, kown_far, kgot, vown_near, vown_far, vgot, q, k, v, dm, probs, small, dkt, dvt,
+                 kown_near, kown_far, kgot, vown_near, vown_far, vgot, q, k, v, dm, probs, dscore, small, dkt, dvt,
                  outs, half_a, full_a, half_b, full_b, half2_a, full2_a, half2_b, full2_b,
                  pair_got, ring_half, ring_full,
                  load_sem, tree_send, tree_recv, ring_send, ring_recv, pair_send, pair_recv,
@@ -356,38 +357,49 @@
 
     scale = 1.0 / math.sqrt(HD)
     pairs = [(c, h, slice(64 * c, 64 * c + 64), slice(128 * h, 128 * h + 128)) for c in range(4) for h in range(2)]
+    scores = [lax.dot_general(q[t, e], k[c, :, e], NT, preferred_element_type=f32) * scale for c, h, t, e in pairs]
+    for (c, h, t, e), s in zip(pairs, scores):
+        p = jnp.exp(s - jnp.max(s, axis=-1, keepdims=True))
+        probs[c, h] = p / jnp.sum(p, axis=-1, keepdims=True)
     for c, h, t, e in pairs:
-        s = lax.dot_general(q[t, e], k[c, :, e], NT, preferred_element_type=f32) * scale
-        p = jnp.exp(s - jnp.max(s, axis=-1, keepdims=True))
-        p = p / jnp.sum(p, axis=-1, keepdims=True)
-        probs[c, h] = p
-        small[0, t, e] = jnp.dot(p.astype(bf), v[c, :, e], preferred_element_type=f32).astype(bf)
+        small[0, t, e] = jnp.dot(probs[c, h].astype(bf), v[c, :, e], preferred_element_type=f32).astype(bf)
     small[2] = small[0].astype(f32).T.astype(bf)
 
     def backward():
-        for c, h, t, e in pairs:
-            p = probs[c, h]
-            dprob = lax.dot_general(dm[t, e], v[c, :, e], NT, preferred_element_type=f32)
-            ds = (p * (dprob - jnp.sum(dprob * p, axis=-1, keepdims=True)) * scale).astype(bf)
-            small[1, t, e] = jnp.dot(ds, k[c, :, e], preferred_element_type=f32).astype(bf)
-            dkt[e, 256 * c:256 * c + 256] = lax.dot_general(q[t, e], ds, TN, preferred_element_type=f32).astype(bf)
-            dvt[e, 256 * c:256 * c + 256] = lax.dot_general(dm[t, e], p.astype(bf), TN, preferred_element_type=f32).astype(bf)
+        dprobs = [lax.dot_general(dm[t, e], v[c, :, e], NT, preferred_element_type=f32) for c, h, t, e in pairs]
+        for i, (c, h, t, e) in enumerate(pairs):
+            p, dprob = probs[c, h], dprobs[i]
+            dscore[i] = (p * (dprob - jnp.sum(dprob * p, axis=-1, keepdims=True)) * scale).astype(bf)
+        for i, (c, h, t, e) in enumerate(pairs):
+            small[1, t, e] = jnp.dot(dscore[i], k[c, :, e], preferred_element_type=f32).astype(bf)
         small[3] = small[1].astype(f32).T.astype(bf)
 
-    def fill_flat(place_of, left, right):
-        def step(j, carry):
+    def backward_rows():
+        for i, (c, h, t, e) in enumerate(pairs):
+            keys = slice(256 * c, 256 * c + 256)
+            dvt[e, keys] = lax.dot_general(dm[t, e], probs[c, h].astype(bf), TN, preferred_element_type=f32).astype(bf)
+            dkt[e, keys] = lax.dot_general(q[t, e], dscore[i], TN, preferred_element_type=f32).astype(bf)
+
+    def nth(i):
+        a = jnp.where(i < 4, i, jnp.where(i < 7, 0, 1 + (i - 7) // 3))
+        b = jnp.where(i < 4, 0, jnp.where(i < 7, i - 3, 1 + (i - 7) % 3))
+        return lax.rem(px + 2 + a, 4) * 4 + lax.rem(pz + 2 + b, 4)
+
+    def fill_flat(place_of, left, right, lo=0, hi=16):
+        def step(i, carry):
+            j = nth(i)
             cols = pl.ds(pl.multiple_of(j * 256, 256), 256)
             weights[place_of, j] = jnp.dot(left[...], right[:, cols], preferred_element_type=f32).astype(bf)
             return carry
-        lax.fori_loop(0, 16, step, 0)
-
-    def fill_rows(place_of, left):
-        def step(j, carry):
-            cols = pl.ds(pl.multiple_of(j * 256, 256), 256)
+        lax.fori_loop(lo, hi, step, 0, unroll=hi - lo)
+
+    def fill_rows(place_of, left, lo=0, hi=16):
+        def step(i, carry):
+            cols = pl.ds(pl.multiple_of(nth(i) * 256, 256), 256)
             value = jnp.dot(left[...], x[:, :, cols].reshape(1024, 256), preferred_element_type=f32).astype(bf)
             got[4 * place_of:4 * place_of + 4, :, :, cols] = value.reshape(4, 4, 16, 256)
             return carry
-        lax.fori_loop(0, 16, step, 0)
+        lax.fori_loop(lo, hi, step, 0, unroll=hi - lo)
 
     def fill_out(u, left, w, flip):
         dims = (((1,), (1 if flip else 0,)), ((), ()))
@@ -398,7 +410,7 @@
             cols = pl.ds(pl.multiple_of((j % 2) * 256, 256), 256)
             outs[u, e % 2, e // 2, :, cols] = value.astype(bf)
             return carry
-        lax.fori_loop(0, 16, step, 0)
+        lax.fori_loop(0, 16, step, 0, unroll=8)
 
     ranks = (2, -1, 1, 0)
 
@@ -531,25 +543,33 @@
     remote(got.at[:, pl.ds(0, 2)], got.at[:, pl.ds(0, 2)], pair_send, pair_recv.at[0], sibling).wait_send()
     for copy in swaps + backs:
         copy.wait_send()
-    fill_flat(0, small.at[2], cot)
+    fill_flat(0, small.at[2], cot, 0, 7)
     begin(3)
+    fill_flat(0, small.at[2], cot, 7, 16)
     fill_out(0, small.at[0], 3, False)
     outs0[0]()
     backward()
-    fill_flat(1, small.at[3], tok)
+    fill_flat(1, small.at[3], tok, 0, 7)
     begin(0)
-    then(3, 0, 4)
+    then(3, 0, 2)
+    fill_flat(1, small.at[3], tok, 7, 16)
+    then(3, 2, 4)
+    backward_rows()
     order_rows()
-    fill_rows(0, dvt)
+    fill_rows(0, dvt, 0, 7)
     begin(2)
-    then(0, 0, 4)
+    then(0, 0, 2)
+    fill_rows(0, dvt, 7, 16)
+    then(0, 2, 4)
+    fill_rows(1, dkt, 0, 7)
+    begin(1)
+    then(2, 0, 2)
     outs0[1]()
-    fill_rows(1, dkt)
-    begin(1)
+    fill_rows(1, dkt, 7, 16)
+    then(2, 2, 4)
     then(3, 4, 8)
     fill_out(1, small.at[1], 2, True)
     outs1[0]()
-    then(2, 0, 4)
     outs0[2]()
     then(0, 4, 8)
     then(1, 0, 4)
@@ -605,6 +625,7 @@
             vm((4, 256, 256), bf),
             vm((256, 256), bf),
             vm((4, 2, 64, 256), jnp.float32),
+            vm((8, 64, 256), bf),
             vm((4, 256, 256), bf),
             vm((256, 1024), bf),
             vm((256, 1024), bf),
@@ -660,7 +681,7 @@
 
 
 def body(tokens, store, holder, rows, wq, wk, wv, wo, cotangent):
-    return finish(*layer(holder, rows, store, wk, wv, wq, wo, tokens, cotangent))
+    return finish(*layer(holder.reshape(8), rows, store, wk, wv, wq, wo, tokens, cotangent))
 
 
 def solution(mesh):

time: 136 us -> 125 us (0.919)
  Pallas kernels: 134 us -> 123 us
    pallas_call x1, Pallas kernels: 132 us -> 121 us  [layer(): pl.pallas_call(layer_kernel, out_shape=(jax.ShapeDtypeStruct((2, 256, 512...]
where the time goes in v4:
time: 125 us; the launch traced here: 124 us
  Pallas kernels  123 us (98%)
    pallas_call x1, Pallas kernels, layer(): pl.pallas_call(layer_kernel, out_shape=(jax.ShapeDtypeStruct((2, 256, 512...  121 us

profile of v4, /device:TPU:0, one launch (start us, length us, event | category | flops | bytes accessed | tf_op | source)
XLA Modules:
  0.0 124.1 jit_solution(952219595117385802)
XLA Ops:
  0.6 121.2 %layer.1 = (bf16[2,256,512]{2,1,0:T(8,128)(2,1)}, bf16[4,256,256]{2,1,0:T(8,128)(2,1)}) custom-call(s32[8]{0:T(128)} %bitcast.1, s32[8]{0:T(128)} %rows_in.1, bf16[8,128,4096]{2,1,0:T(8,128)(2,1)} %store.1, bf16[256,256]{1,0:T(8,128)(2,1)} %wk.1, bf16[256,256]{1,0:T(8,128)(2,1)} %wv.1, bf16[256,256]{1,0:T(8,128)(2,1)} %wq.1, bf16[256,256]{1,0:T(8,128)(2,1)} %wo.1, ...), custom_call_target="tpu_custom_call" | custom-call | tf_op jit(solution)/shard_map/layer/pallas_call | solution.py:602
  121.8 2.3 %finish.1 = (bf16[256,512]{1,0:T(8,128)(2,1)}, bf16[256,512]{1,0:T(8,128)(2,1)}, bf16[256,256]{1,0:T(8,128)(2,1)}, bf16[256,256]{1,0:T(8,128)(2,1)}, bf16[256,256]{1,0:T(8,128)(2,1)}, /*index=5*/bf16[256,256]{1,0:T(8,128)(2,1)}) custom-call(bf16[2,256,512]{2,1,0:T(8,128)(2,1)} %get-tuple-element.8.wide, bf16[4,256,256]{2,1,0:T(8,128)(2,1)} %get-tuple-element.9.square), custom_call_target="tpu_custom_call" | custom-call | tf_op jit(solution)/shard_map/finish/pallas_call | solution.py:674

commit v5 on v4

--- a/solution.py
+++ b/solution.py
@@ -248,7 +248,7 @@
     load_cot.start()
     advance(4)
 
-    groups = ((0, 4), (4, 8), (8, 12), (12, 15), (15, 18))
+    groups = ((0, 4), (4, 8), (8, 12), (12, 16), (16, 18))
     group_of = [i for i, (lo, hi) in enumerate(groups) for _ in range(lo, hi)]
 
     def pair_wait(group):
@@ -329,7 +329,7 @@
             remote(ring_ref(u - 2), ring_ref(u - 2), pair_send, pair_recv.at[group_of[u - 2]], sibling).start()
         if u in (2, 3):
             backs[u - 2].start()
-        advance(4 + (total - 4) * (u + 1) // TREE_SPAN)
+        advance(4 + (total - 4) * u // TREE_SPAN)
         if u in work:
             work[u]()
     advance(total)
@@ -563,11 +563,12 @@
     then(0, 2, 4)
     fill_rows(1, dkt, 0, 7)
     begin(1)
+    then(3, 4, 6)
+    fill_rows(1, dkt, 7, 16)
     then(2, 0, 2)
     outs0[1]()
-    fill_rows(1, dkt, 7, 16)
     then(2, 2, 4)
-    then(3, 4, 8)
+    then(3, 6, 8)
     fill_out(1, small.at[1], 2, True)
     outs1[0]()
     outs0[2]()
@@ -580,11 +581,12 @@
     outs1[2]()
     then(0, 8, 10)
     then(1, 4, 8)
+    then(2, 8, 10)
     then(3, 10, 11)
-    then(2, 8, 10)
+    then(1, 8, 9)
+    then(0, 10, 11)
+    then(1, 9, 10)
     outs1[3]()
-    then(0, 10, 11)
-    then(1, 8, 10)
     then(2, 10, 11)
     then(1, 10, 11)
     for t in range(TREES):

time: 125 us -> 121 us (0.968)
  Pallas kernels: 123 us -> 121 us
    pallas_call x1, Pallas kernels: 121 us -> 118 us  [layer(): pl.pallas_call(layer_kernel, out_shape=(jax.ShapeDtypeStruct((2, 256, 512...]
where the time goes in v5:
time: 121 us
  Pallas kernels  121 us (100%)
    pallas_call x1, Pallas kernels, layer(): pl.pallas_call(layer_kernel, out_shape=(jax.ShapeDtypeStruct((2, 256, 512...  118 us

profile of v5, /device:TPU:0, one launch (start us, length us, event | category | flops | bytes accessed | tf_op | source)
XLA Modules:
  0.0 121.3 jit_solution(6371412582814075626)
XLA Ops:
  0.6 118.4 %layer.1 = (bf16[2,256,512]{2,1,0:T(8,128)(2,1)}, bf16[4,256,256]{2,1,0:T(8,128)(2,1)}) custom-call(s32[8]{0:T(128)} %bitcast.1, s32[8]{0:T(128)} %rows_in.1, bf16[8,128,4096]{2,1,0:T(8,128)(2,1)} %store.1, bf16[256,256]{1,0:T(8,128)(2,1)} %wk.1, bf16[256,256]{1,0:T(8,128)(2,1)} %wv.1, bf16[256,256]{1,0:T(8,128)(2,1)} %wq.1, bf16[256,256]{1,0:T(8,128)(2,1)} %wo.1, ...), custom_call_target="tpu_custom_call" | custom-call | tf_op jit(solution)/shard_map/layer/pallas_call | solution.py:604
  119.0 2.3 %finish.1 = (bf16[256,512]{1,0:T(8,128)(2,1)}, bf16[256,512]{1,0:T(8,128)(2,1)}, bf16[256,256]{1,0:T(8,128)(2,1)}, bf16[256,256]{1,0:T(8,128)(2,1)}, bf16[256,256]{1,0:T(8,128)(2,1)}, /*index=5*/bf16[256,256]{1,0:T(8,128)(2,1)}) custom-call(bf16[2,256,512]{2,1,0:T(8,128)(2,1)} %get-tuple-element.8.wide, bf16[4,256,256]{2,1,0:T(8,128)(2,1)} %get-tuple-element.9.square), custom_call_target="tpu_custom_call" | custom-call | tf_op jit(solution)/shard_map/finish/pallas_call | solution.py:676

commit v6 on v5

--- a/solution.py
+++ b/solution.py
@@ -360,7 +360,7 @@
     scores = [lax.dot_general(q[t, e], k[c, :, e], NT, preferred_element_type=f32) * scale for c, h, t, e in pairs]
     for (c, h, t, e), s in zip(pairs, scores):
         p = jnp.exp(s - jnp.max(s, axis=-1, keepdims=True))
-        probs[c, h] = p / jnp.sum(p, axis=-1, keepdims=True)
+        probs[c, h] = p * (1.0 / jnp.sum(p, axis=-1, keepdims=True))
     for c, h, t, e in pairs:
         small[0, t, e] = jnp.dot(probs[c, h].astype(bf), v[c, :, e], preferred_element_type=f32).astype(bf)
     small[2] = small[0].astype(f32).T.astype(bf)
@@ -663,12 +663,23 @@
     )(holder, rows, store, wk, wv, wq, wo, tokens, cotangent)
 
 
-def finish_kernel(wide, square, cca, gtok, gq, gk, gv, go_out):
-    cca[...] = wide[0]
-    gtok[...] = wide[1]
-    for w, out in ((0, gq), (1, gk), (2, gv)):
-        out[...] = square[w].astype(jnp.float32).T.astype(jnp.bfloat16)
-    go_out[...] = square[3]
+def finish_kernel(wide, square, cca, gtok, gq, gk, gv, go_out, wide_held, square_held, flipped, load_sem, save_sem):
+    parts = [(square.at[i], square_held.at[i], flipped.at[i], out) for i, out in enumerate((gq, gk, gv))]
+    parts += [(square.at[3], square_held.at[3], None, go_out)]
+    parts += [(wide.at[i], wide_held.at[i], None, out) for i, out in enumerate((cca, gtok))]
+    loads = [pltpu.make_async_copy(src, held, load_sem.at[i]) for i, (src, held, _, _) in enumerate(parts)]
+    for copy in loads:
+        copy.start()
+    saves = []
+    for i, (_, held, turned, out) in enumerate(parts):
+        loads[i].wait()
+        if turned is not None:
+            turned[...] = held[...].astype(jnp.float32).T.astype(jnp.bfloat16)
+        save = pltpu.make_async_copy(held if turned is None else turned, out, save_sem.at[i])
+        save.start()
+        saves.append(save)
+    for copy in saves:
+        copy.wait()
 
 
 def finish(wide, square):
@@ -676,8 +687,10 @@
     return pl.pallas_call(
         finish_kernel,
         out_shape=(jax.ShapeDtypeStruct((256, 512), bf),) * 2 + (jax.ShapeDtypeStruct((256, 256), bf),) * 4,
-        in_specs=[VMEM] * 2,
-        out_specs=(VMEM,) * 6,
+        in_specs=[ANY] * 2,
+        out_specs=(ANY,) * 6,
+        scratch_shapes=[pltpu.VMEM((2, 256, 512), bf), pltpu.VMEM((4, 256, 256), bf), pltpu.VMEM((3, 256, 256), bf),
+                        pltpu.SemaphoreType.DMA((6,)), pltpu.SemaphoreType.DMA((6,))],
         name="finish",
     )(wide, square)
 

time: 121 us -> 122 us (level)
  no operation moved by 1% of the time
where the time goes in v6:
time: 122 us; the launch traced here: 121 us
  Pallas kernels  121 us (99%)
    pallas_call x1, Pallas kernels, layer(): pl.pallas_call(layer_kernel, out_shape=(jax.ShapeDtypeStruct((2, 256, 512...  118 us

profile of v6, /device:TPU:0, one launch (start us, length us, event | category | flops | bytes accessed | tf_op | source)
XLA Modules:
  0.0 121.4 jit_solution(17754794342902608518)
XLA Ops:
  0.6 118.4 %layer.1 = (bf16[2,256,512]{2,1,0:T(8,128)(2,1)}, bf16[4,256,256]{2,1,0:T(8,128)(2,1)}) custom-call(s32[8]{0:T(128)} %bitcast.1, s32[8]{0:T(128)} %rows_in.1, bf16[8,128,4096]{2,1,0:T(8,128)(2,1)} %store.1, bf16[256,256]{1,0:T(8,128)(2,1)} %wk.1, bf16[256,256]{1,0:T(8,128)(2,1)} %wv.1, bf16[256,256]{1,0:T(8,128)(2,1)} %wq.1, bf16[256,256]{1,0:T(8,128)(2,1)} %wo.1, ...), custom_call_target="tpu_custom_call" | custom-call | tf_op jit(solution)/shard_map/layer/pallas_call | solution.py:604
  119.0 2.2 %finish.1 = (bf16[256,512]{1,0:T(8,128)(2,1)}, bf16[256,512]{1,0:T(8,128)(2,1)}, bf16[256,256]{1,0:T(8,128)(2,1)}, bf16[256,256]{1,0:T(8,128)(2,1)}, bf16[256,256]{1,0:T(8,128)(2,1)}, /*index=5*/bf16[256,256]{1,0:T(8,128)(2,1)}) custom-call(bf16[2,256,512]{2,1,0:T(8,128)(2,1)} %get-tuple-element.8.wide, bf16[4,256,256]{2,1,0:T(8,128)(2,1)} %get-tuple-element.9.square), custom_call_target="tpu_custom_call" | custom-call | tf_op jit(solution)/shard_map/finish/pallas_call | solution.py:687
